TPU v7x, 256 devices: a whole 4x4x8 slice. The times are simulated.
256 devices in a mesh: gx: 8 (over z), gy: 8 (over y_hi, x), gz: 4 (over y_lo, core).
Axes of the slice: x: 4, y: 4 (y_hi: 2, y_lo: 2; y = y_hi * 2 + y_lo), z: 8, core: 2. Of those that a mesh axis runs over, the one named last changes fastest.
Arguments:
- incumbent_wavenumber_normals: float32 [2, 256, 512, 512], P(None, ('gy', 'gz'), 'gx'), may hold values from -6 to 6
- renewed_wavenumber_normals: float32 [2, 256, 512, 512], P(None, ('gy', 'gz'), 'gx'), may hold values from -6 to 6
- jump_scale_factor: float32 [1], replicated, may hold values from 0.2 to 0.6
- unsintered_solidity: float32 [256, 512, 512], P('gx', 'gy', 'gz'), may hold values from 0.45 to 0.8
- opening_warmth_map: float32 [256, 512, 512], P('gx', 'gy', 'gz'), may hold values from 0.7 to 1.3
- detector_lattice_place: int32 [4096, 3], replicated, may hold values from 0 to 511, as said below
- recorded_detector_kelvin: float32 [4096], replicated, may hold values from 0.8 to 1.4
- incumbent_mismatch_cost: float32 [1], replicated, may hold values from 1 to 3
Outputs:
- suggested_arrhenius_threshold: float32 [256, 512, 512], P('gx', 'gy', 'gz')
- density: float32 [256, 512, 512], P('gx', 'gy', 'gz')
- ending_kelvin_array: float32 [256, 512, 512], P('gx', 'gy', 'gz')
- modelled_detector_kelvin: float32 [4096], replicated
- natural_admit_odds: float32 [1], replicated
Inputs may be any that keep to these rules, and one draw needn't show every extreme that they name: `detector_lattice_place`: each row holds one sensor's cell as (x, y, z) with x below 256, y below 512 and z below 512; sensors may share a cell.
All inputs are finite; a program needn't handle non-finite values.
Results may differ from a plain program's by a relative error of at most 0.000094.
Values sent between devices are 32-bit elements; how exact they have to be, the bound alone decides.
A program may use at most 128 MiB of HBM per device.

v0:
```python
import math

import jax
import jax.numpy as jnp
from jax import lax
from jax.sharding import PartitionSpec as P

MESH_EXTENT_EAST = 256
MESH_EXTENT_NORTH = 512
MESH_EXTENT_UPWARD = 512
STEPS = 3


def padded_2(cells, sides, width):
    for axis, dim in sides:
        count = lax.axis_size(axis)
        ends = count - 1
        head = lax.slice_in_dim(cells, 0, width, axis=dim)
        tail = lax.slice_in_dim(cells, cells.shape[dim] - width, cells.shape[dim], axis=dim)
        cells = jnp.concatenate(
            [
                lax.ppermute(tail, axis, [(i, (i + 1) % count) for i in range(ends)]),
                cells,
                lax.ppermute(head, axis, [((i + 1) % count, i) for i in range(ends)]),
            ],
            axis=dim,
        )
    return cells


def spectrum(length):
    wave = jnp.arange(length, dtype=jnp.int32)
    signed = jnp.where(wave < length // 2, wave, wave - length).astype(jnp.float32)
    shape = 1.0 / jnp.sqrt(1.0 + (signed / 8.0) ** 2)
    return shape / jnp.sqrt(jnp.sum(shape * shape))


def twiddle(waves, length):
    places = jnp.arange(length, dtype=jnp.int32)
    phase = waves[:, None] * places[None, :] % length
    angle = phase.astype(jnp.float32) * (2.0 * math.pi / length)
    return (jnp.cos(angle), jnp.sin(angle))


def inverse_axis(real, imag, cosine, sine, form):
    highest = lax.Precision.HIGHEST
    real_cos = jnp.einsum(form, real, cosine, precision=highest)
    imag_sin = jnp.einsum(form, imag, sine, precision=highest)
    real_sin = jnp.einsum(form, real, sine, precision=highest)
    imag_cos = jnp.einsum(form, imag, cosine, precision=highest)
    return (real_cos - imag_sin, real_sin + imag_cos)


def neighbours(padded):
    return [
        padded[2:, 1:-1, 1:-1],
        padded[:-2, 1:-1, 1:-1],
        padded[1:-1, 2:, 1:-1],
        padded[1:-1, :-2, 1:-1],
        padded[1:-1, 1:-1, 2:],
        padded[1:-1, 1:-1, :-2],
    ]


def march_forward(heat_pad, solidity_margined, barrier_inner):
    warmth_map_components = heat_pad[1:-1, 1:-1, 1:-1]
    fractional_packing = solidity_margined[1:-1, 1:-1, 1:-1]
    conduct_pad = solidity_margined * solidity_margined
    conduct = conduct_pad[1:-1, 1:-1, 1:-1]
    conductive_stream = jnp.zeros_like(warmth_map_components)
    for heat_side, cond_side in zip(neighbours(heat_pad), neighbours(conduct_pad)):
        conductive_stream = conductive_stream + 0.5 * (conduct + cond_side) * (
            heat_side - warmth_map_components
        )
    densify_rate = jnp.exp(-barrier_inner / (warmth_map_components + 1.25)) * (
        1.0 - fractional_packing
    )
    return (
        warmth_map_components + 0.16 * (conductive_stream + 3.0 * densify_rate),
        fractional_packing + 0.64 * densify_rate,
    )


def body(
    incumbent_wavenumber_normals,
    renewed_wavenumber_normals,
    jump_scale_factor,
    unsintered_solidity,
    opening_warmth_map,
    detector_lattice_place,
    recorded_detector_kelvin,
    incumbent_mismatch_cost,
):
    beta = jump_scale_factor[0]
    mixed = (
        jnp.sqrt(1.0 - beta * beta) * incumbent_wavenumber_normals
        + beta * renewed_wavenumber_normals
    )
    piece_x = mixed.shape[1]
    piece_y = mixed.shape[2]
    scale_x = lax.dynamic_slice_in_dim(
        spectrum(MESH_EXTENT_EAST), lax.axis_index(("gy", "gz")) * piece_x, piece_x
    )
    scale_y = lax.dynamic_slice_in_dim(
        spectrum(MESH_EXTENT_NORTH), lax.axis_index("gx") * piece_y, piece_y
    )
    amplitude = (
        scale_x[:, None, None]
        * scale_y[None, :, None]
        * spectrum(MESH_EXTENT_UPWARD)[None, None, :]
    )
    depth_cos, depth_sin = twiddle(
        jnp.arange(MESH_EXTENT_UPWARD, dtype=jnp.int32), MESH_EXTENT_UPWARD
    )
    real, imag = inverse_axis(
        mixed[0] * amplitude, mixed[1] * amplitude, depth_cos, depth_sin, "xyk,kn->xyn"
    )
    stacked = lax.all_to_all(jnp.stack([real, imag]), "gx", split_axis=3, concat_axis=2, tiled=True)
    width_cos, width_sin = twiddle(
        jnp.arange(MESH_EXTENT_NORTH, dtype=jnp.int32), MESH_EXTENT_NORTH
    )
    real, imag = inverse_axis(stacked[0], stacked[1], width_cos, width_sin, "xkz,kn->xnz")
    stacked = jnp.stack([real, imag])
    stacked = lax.all_to_all(stacked, ("gy", "gz"), split_axis=2, concat_axis=1, tiled=True)
    waves_x = jnp.arange(MESH_EXTENT_EAST, dtype=jnp.int32)
    first_cos, first_sin = twiddle(waves_x, MESH_EXTENT_EAST)
    highest = lax.Precision.HIGHEST
    field = jnp.einsum("kyz,kn->nyz", stacked[0], first_cos, precision=highest) - jnp.einsum(
        "kyz,kn->nyz", stacked[1], first_sin, precision=highest
    )
    energy_pencil = 2.0 + 0.6 * jnp.tanh(field)
    suggested_arrhenius_threshold = lax.all_to_all(
        lax.all_to_all(energy_pencil, "gx", split_axis=0, concat_axis=2, tiled=True),
        "gz",
        split_axis=2,
        concat_axis=1,
        tiled=True,
    )
    warmth_map_components = opening_warmth_map - 1.25
    fractional_packing = unsintered_solidity
    block_x, block_y, block_z = warmth_map_components.shape
    for step in range(STEPS):
        padded = padded_2(
            jnp.stack([warmth_map_components, fractional_packing]),
            (("gx", 1), ("gy", 2), ("gz", 3)),
            1,
        )
        warmth_map_components, fractional_packing = march_forward(
            padded[0], padded[1], suggested_arrhenius_threshold
        )
    ending_kelvin_array = warmth_map_components + 1.25
    local_x = detector_lattice_place[:, 0] - lax.axis_index("gx") * block_x
    local_y = detector_lattice_place[:, 1] - lax.axis_index("gy") * block_y
    local_z = detector_lattice_place[:, 2] - lax.axis_index("gz") * block_z
    probe_locality_flags = (
        (local_x >= 0)
        & (local_x < block_x)
        & (local_y >= 0)
        & (local_y < block_y)
        & (local_z >= 0)
        & (local_z < block_z)
    )
    flattened_cell_offset = (
        jnp.clip(local_x, 0, block_x - 1) * block_y + jnp.clip(local_y, 0, block_y - 1)
    ) * block_z + jnp.clip(local_z, 0, block_z - 1)
    detector_inside_subdomain = jnp.where(
        probe_locality_flags, ending_kelvin_array.reshape(-1)[flattened_cell_offset], 0.0
    )
    modelled_detector_kelvin = lax.psum(detector_inside_subdomain, ("gx", "gy", "gz"))
    residual_sumsq = 0.5 * jnp.mean(
        ((modelled_detector_kelvin - recorded_detector_kelvin) / 0.2) ** 2
    )
    natural_admit_odds = incumbent_mismatch_cost - residual_sumsq
    return (
        suggested_arrhenius_threshold,
        fractional_packing,
        ending_kelvin_array,
        modelled_detector_kelvin,
        natural_admit_odds,
    )


def solution(mesh):
    return jax.shard_map(
        body,
        mesh=mesh,
        in_specs=(
            P(None, ("gy", "gz"), "gx", None),
            P(None, ("gy", "gz"), "gx", None),
            P(),
            P("gx", "gy", "gz"),
            P("gx", "gy", "gz"),
            P(),
            P(),
            P(),
        ),
        out_specs=(P("gx", "gy", "gz"), P("gx", "gy", "gz"), P("gx", "gy", "gz"), P(), P()),
        check_vma=False,
    )
```

profile of v0, /device:TPU:1, one launch (start us, length us, event | category | flops | bytes accessed | tf_op | source)
XLA Modules:
  0.0 544.4 jit_solution(16666940818359520167)
XLA Ops:
  6.9 5.8 %fusion.72 = f32[8,64,512]{2,1,0:T(8,128)S(1)} fusion(f32[2,8,64,512]{3,2,1,0:T(8,128)S(1)} %multiply_add_fusion, f32[512]{0:T(512)S(1)} %fusion.116, f32[8,64]{1,0:T(8,128)S(1)} %broadcast_multiply_fusion), kind=kOutput, calls=%fused_computation.134 | convolution fusion | flops 1614807040 | bytes 2103296 | tf_op jit(solution)/shard_map/xyk,kn->xyn/dot_general | solution.py:47
  12.7 6.0 %fusion.68 = f32[8,64,512]{2,1,0:T(8,128)S(1)} fusion(f32[2,8,64,512]{3,2,1,0:T(8,128)S(1)} %multiply_add_fusion, f32[512]{0:T(512)S(1)} %fusion.116, f32[8,64]{1,0:T(8,128)S(1)} %broadcast_multiply_fusion), kind=kOutput, calls=%fused_computation.130 | convolution fusion | flops 1614807040 | bytes 2103296 | tf_op jit(solution)/shard_map/xyk,kn->xyn/dot_general | solution.py:49
  18.7 5.8 %fusion.1 = f32[1,8,64,512]{3,2,1,0:T(8,128)S(1)} fusion(f32[8,64,512]{2,1,0:T(8,128)S(1)} %fusion.72, f32[2,8,64,512]{3,2,1,0:T(8,128)S(1)} %multiply_add_fusion, f32[512]{0:T(512)S(1)} %fusion.116, f32[8,64]{1,0:T(8,128)S(1)} %broadcast_multiply_fusion), kind=kOutput, calls=%fused_computation.25 | convolution fusion | flops 1615069184 | bytes 3151872 | tf_op jit(solution)/shard_map/xyk,kn->xyn/dot_general | solution.py:48
  24.5 6.0 %fusion = f32[1,8,64,512]{3,2,1,0:T(8,128)S(1)} fusion(f32[8,64,512]{2,1,0:T(8,128)S(1)} %fusion.68, f32[2,8,64,512]{3,2,1,0:T(8,128)S(1)} %multiply_add_fusion, f32[512]{0:T(512)S(1)} %fusion.116, f32[8,64]{1,0:T(8,128)S(1)} %broadcast_multiply_fusion), kind=kOutput, calls=%fused_computation.23 | convolution fusion | flops 1615069184 | bytes 3151872 | tf_op jit(solution)/shard_map/xyk,kn->xyn/dot_general | solution.py:50
  30.7 3.8 copy.61
  34.5 5.9 %reshape.114 = f32[8,1,65536]{2,1,0:T(1,128)S(1)} reshape(f32[512,2,8,64]{3,2,1,0:T(8,128)} %bitcast.131) | data formatting | bytes 4194304
  40.4 58.6 %all_to_all.66 = f32[8,1,65536]{2,1,0:T(1,128)} all-to-all(f32[8,1,65536]{2,1,0:T(1,128)S(1)} %reshape.114), channel_id=1, replica_groups=mesh['gx'=8,'gy'=8,'gz'=4] {'gx'}, dimensions={0} | all-to-all | bytes 4194304 | tf_op jit(solution)/shard_map/all_to_all | solution.py:118
  99.6 7.2 %reduce.2 = f32[8,65536]{1,0:T(8,128)S(1)} reduce(f32[8,1,65536]{2,1,0:T(1,128)} %all_to_all.66, f32[]{:T(128)} %broadcast.281), dimensions={1}, to_apply=%all_to_all.48.reduce_sub_computation | reduce | bytes 4194308 | tf_op jit(solution)/shard_map/all_to_all | solution.py:118
  106.8 3.6 reshape.115
  110.4 4.6 copy.90
  118.7 7.0 %fusion.88 = f32[512,512]{0,1} fusion(f32[512,512]{0,1:T(8,128)S(1)} %bitcast.149), kind=kOutput, calls=%fused_computation.159 | convolution fusion | flops 1614282752 | bytes 2097152
  125.7 6.6 %fusion.96 = f32[512,512]{0,1} fusion(f32[512,512]{0,1:T(8,128)S(1)} %bitcast.150), kind=kOutput, calls=%fused_computation.162 | convolution fusion | flops 1614282752 | bytes 2097152
  132.8 6.4 %fusion.94 = f32[512,512]{0,1:S(1)} fusion(f32[512,512]{0,1:T(8,128)S(1)} %bitcast.151), kind=kOutput, calls=%fused_computation.161 | convolution fusion | flops 1614282752 | bytes 2097152
  139.2 6.5 %fusion.90 = f32[512,512]{0,1:S(1)} fusion(f32[512,512]{0,1:T(8,128)S(1)} %bitcast.152), kind=kOutput, calls=%fused_computation.160 | convolution fusion | flops 1614282752 | bytes 2097152
  146.5 3.8 copy.63
  150.3 4.5 reshape.116
  154.8 38.5 %all_to_all.67 = f32[32,1,16384]{2,1,0:T(1,128)} all-to-all(f32[32,1,16384]{2,1,0:T(1,128)S(1)} %reshape.116), channel_id=1, replica_groups=mesh['gx'=8,'gy'=8,'gz'=4] {'gy','gz'}, dimensions={0} | all-to-all | bytes 4194304 | tf_op jit(solution)/shard_map/all_to_all | solution.py:124
  193.3 7.4 %reduce.3 = f32[32,16384]{1,0:T(8,128)S(1)} reduce(f32[32,1,16384]{2,1,0:T(1,128)} %all_to_all.67, f32[]{:T(128)} %broadcast.281), dimensions={1}, to_apply=%all_to_all.51.reduce_sub_computation | reduce | bytes 4194308 | tf_op jit(solution)/shard_map/all_to_all | solution.py:124
  200.7 3.4 reshape.117
  204.2 3.5 copy.64
  220.6 4.4 all-to-all-start.2
  225.1 3.2 collective-permute-start
  229.7 16.8 %collective-permute-done = f32[2,1,64,128]{3,2,1,0:T(8,128)S(1)} collective-permute-done((f32[2,1,64,128]{3,2,1,0:T(8,128)S(1)}, f32[2,1,64,128]{3,2,1,0:T(8,128)S(1)}, u32[]{:S(2)}, u32[]{:S(2)}) %collective-permute-start) | collective-permute-done | bytes 65568 | tf_op jit(solution)/shard_map/ppermute | solution.py:22
  246.5 3.4 collective-permute-done.1
  252.6 3.9 collective-permute-done.3
  262.5 5.3 collective-permute-start.4
  278.0 4.4 reduce.4
  284.5 4.4 copy.86
  288.9 4.8 reshape.120
  293.7 4.2 all-to-all-start.3
  297.9 6.8 %pad_maximum_fusion = f32[2,34,66,130]{3,2,1,0:T(8,128)S(1)} fusion(f32[2,34,66,1]{3,2,1,0:T(8,128)} %copy.77, f32[2,34,1,128]{3,2,1,0:T(1,128)S(1)} %collective-permute-done.3, f32[2,1,64,128]{3,2,1,0:T(8,128)S(1)} %collective-permute-done.1, f32[1,32,64,128]{3,2,1,0:T(8,128)S(1)} %bitcast.140, f32[1,32,64,128]{3,2,1,0:T(8,128)S(1)} %add_bitcast_fusion.2, ...), kind=kLoop, calls=%fused_computation.1 | loop fusion | flops 4084080 | bytes 4667520 | tf_op jit(solution)/shard_map/concatenate | solution.py:20
  308.8 4.6 reduce.5
  313.4 3.4 reshape.121
  316.9 3.4 copy.87
  320.4 10.9 %fusion.52 = (f32[1,32,64,128]{3,2,1,0:T(8,128)S(1)}, f32[1,32,64,128]{3,2,1,0:T(8,128)S(1)}) fusion(f32[34,66,130]{2,1,0:T(8,128)} %get-tuple-element.15, f32[34,66,130]{2,1,0:T(8,128)S(1)} %fusion.162, f32[34,66,130]{2,1,0:T(8,128)} %get-tuple-element.16, f32[32,4,16,128]{3,2,1,0:T(8,128)S(1)} %copy.73), kind=kLoop, calls=%fused_computation.101 | loop fusion | flops 10485760 | bytes 18874368 | tf_op jit(solution)/shard_map/stack | solution.py:144
  334.0 3.8 collective-permute-done.7
  351.8 5.9 %collective-permute-start.10 = (f32[2,34,66,1]{2,0,3,1:T(2,128)}, f32[2,34,66,1]{2,0,3,1:T(2,128)}, u32[]{:S(2)}, u32[]{:S(2)}) collective-permute-start(f32[2,34,66,1]{2,0,3,1:T(2,128)} %copy.78), channel_id=1, source_target_pairs={{0,1},{1,2},{2,3},{4,5},{5,6},{6,7},{8,9},{9,10},{10,11},{12,13},{... | collective-permute-start | bytes 53864 | tf_op jit(solution)/shard_map/ppermute | solution.py:22
  367.0 6.8 %pad_maximum_fusion.1 = f32[2,34,66,130]{3,2,1,0:T(8,128)S(1)} fusion(f32[2,34,66,1]{3,2,1,0:T(8,128)} %copy.81, f32[2,34,1,128]{3,2,1,0:T(1,128)S(1)} %copy-done.19, f32[2,1,64,128]{3,2,1,0:T(8,128)S(1)} %copy-done.14, f32[1,32,64,128]{3,2,1,0:T(8,128)S(1)} %copy-done.2, f32[1,32,64,128]{3,2,1,0:T(8,128)S(1)} %get-tuple-element.9, ...), kind=kLoop, calls=%fused_computation.2 | loop fusion | flops 4084080 | bytes 4667520 | tf_op jit(solution)/shard_map/concatenate | solution.py:20
  375.5 4.0 fusion.31
  379.6 5.6 %collective-permute-start.12 = (f32[2,1,64,128]{3,2,1,0:T(8,128)S(1)}, f32[2,1,64,128]{3,2,1,0:T(8,128)S(1)}, u32[]{:S(2)}, u32[]{:S(2)}) collective-permute-start(f32[2,1,64,128]{3,2,1,0:T(8,128)S(1)} %get-tuple-element.33), channel_id=1, source_target_pairs={{0,32},{32,64},{64,96},{96,128},{128,160},{160,192},{192,224},{1,3... | collective-permute-start | bytes 196616 | tf_op jit(solution)/shard_map/ppermute | solution.py:22
  387.0 4.2 collective-permute-done.13
  391.2 6.7 %collective-permute-start.14 = (f32[2,34,1,128]{3,2,1,0:T(1,128)S(1)}, f32[2,34,1,128]{3,2,1,0:T(1,128)S(1)}, u32[]{:S(2)}, u32[]{:S(2)}) collective-permute-start(f32[2,34,1,128]{3,2,1,0:T(1,128)S(1)} %get-tuple-element.27), channel_id=1, source_target_pairs={{0,4},{4,8},{8,12},{12,16},{16,20},{20,24},{24,28},{1,5},{5,9},{9,... | collective-permute-start | bytes 104456 | tf_op jit(solution)/shard_map/ppermute | solution.py:22
  399.3 3.6 collective-permute-done.15
  408.9 5.0 collective-permute-start.16
  424.9 6.8 %pad_maximum_fusion.2 = f32[2,34,66,130]{3,2,1,0:T(8,128)S(1)} fusion(f32[2,34,66,1]{3,2,1,0:T(8,128)} %copy.85, f32[2,34,1,128]{3,2,1,0:T(1,128)S(1)} %collective-permute-done.15, f32[2,1,64,128]{3,2,1,0:T(8,128)S(1)} %collective-permute-done.13, f32[1,32,64,128]{3,2,1,0:T(8,128)S(1)} %get-tuple-element.8, f32[1,32,64,128]{3,2,1,0:T(8,128)S(1)} %get-tuple-element.7, ...), kind=kLoop, calls=%fused_computation.3 | loop fusion | flops 4084080 | bytes 4667520 | tf_op jit(solution)/shard_map/concatenate | solution.py:20
  432.3 4.8 fusion.10
  437.1 23.0 %gather_fusion = f32[4096]{0:T(1024)S(1)} fusion(f32[262144]{0:T(1024)S(1)} %bitcast.127, s32[4096]{0:T(1024)S(1)} %broadcast_clamp_fusion), kind=kCustom, calls=%fused_computation | custom fusion | bytes 49152 | tf_op jit(solution)/shard_map/gather | solution.py:167
  460.2 81.4 %psum.7 = f32[4096]{0:T(1024)S(1)} all-reduce(f32[4096]{0:T(1024)S(1)} %broadcast_select_fusion), channel_id=1, replica_groups=mesh['gx'=8,'gy'=8,'gz'=4] {'gx','gy','gz'}, use_global_device_ids=true, to_apply=%region_2.3 | all-reduce | flops 4096 | bytes 32768 | tf_op jit(solution)/shard_map/psum | solution.py:169
  (133 shorter events, 97.2 us)
Async XLA Ops:
  139.2 6.5 %copy-start.9 = (f32[512,512]{0,1:S(1)}, f32[512,512]{0,1}, u32[]{:S(2)}) copy-start(f32[512,512]{0,1} %fusion.88) | copy-start | bytes 3145732
  139.2 6.5 %copy-start.10 = (f32[512,512]{0,1:S(1)}, f32[512,512]{0,1}, u32[]{:S(2)}) copy-start(f32[512,512]{0,1} %fusion.96) | copy-start | bytes 3145732
  210.7 3.0 copy-start.6
  215.0 2.0 copy-start.7
  218.5 6.5 %copy-start.8 = (f32[32,64,128]{2,1,0:T(8,128)S(1)}, f32[32,64,128]{2,1,0:T(8,128)}, u32[]{:S(2)}) copy-start(f32[32,64,128]{2,1,0:T(8,128)} %param.12) | copy-start | bytes 3145732
  220.6 4.5 copy-start.5
  220.6 57.4 %all-to-all-start.2 = ((f32[8,1,32768]{2,1,0:T(1,128)}), f32[8,1,32768]{2,1,0:T(1,128)}, u32[]{:S(2)}, u32[]{:S(2)}) async-start(f32[8,1,32768]{2,1,0:T(1,128)} %reshape.118), calls=%async_computation.2 | async-start | bytes 2097152 | tf_op jit(solution)/shard_map/all_to_all | solution.py:133
  225.1 21.4 %collective-permute-start = (f32[2,1,64,128]{3,2,1,0:T(8,128)S(1)}, f32[2,1,64,128]{3,2,1,0:T(8,128)S(1)}, u32[]{:S(2)}, u32[]{:S(2)}) collective-permute-start(f32[2,1,64,128]{3,2,1,0:T(8,128)S(1)} %get-tuple-element.37), channel_id=1, source_target_pairs={{0,32},{32,64},{64,96},{96,128},{128,160},{160,192},{192,224},{1,3... | collective-permute-start | bytes 196616 | tf_op jit(solution)/shard_map/ppermute | solution.py:22
  228.4 21.6 %collective-permute-start.1 = (f32[2,1,64,128]{3,2,1,0:T(8,128)S(1)}, f32[2,1,64,128]{3,2,1,0:T(8,128)S(1)}, u32[]{:S(2)}, u32[]{:S(2)}) collective-permute-start(f32[2,1,64,128]{3,2,1,0:T(8,128)S(1)} %get-tuple-element.38), channel_id=1, source_target_pairs={{32,0},{64,32},{96,64},{128,96},{160,128},{192,160},{224,192},{33,... | collective-permute-start | bytes 196616 | tf_op jit(solution)/shard_map/ppermute | solution.py:24
  250.0 2.6 collective-permute-start.2
  251.3 5.2 collective-permute-start.3
  262.5 9.8 %collective-permute-start.4 = (f32[2,34,66,1]{2,0,3,1:T(2,128)S(1)}, f32[2,34,66,1]{2,0,3,1:T(2,128)S(1)}, u32[]{:S(2)}, u32[]{:S(2)}) collective-permute-start(f32[2,34,66,1]{2,0,3,1:T(2,128)S(1)} %copy.74), channel_id=1, source_target_pairs={{0,1},{1,2},{2,3},{4,5},{5,6},{6,7},{8,9},{9,10},{10,11},{12,13},{... | collective-permute-start | bytes 53864 | tf_op jit(solution)/shard_map/ppermute | solution.py:22
  270.4 5.3 collective-permute-start.5
  293.7 15.1 %all-to-all-start.3 = ((f32[4,1,65536]{2,1,0:T(1,128)}), f32[4,1,65536]{2,1,0:T(1,128)}, u32[]{:S(2)}, u32[]{:S(2)}) async-start(f32[4,1,65536]{2,1,0:T(1,128)} %reshape.120), calls=%async_computation.3 | async-start | bytes 2097152 | tf_op jit(solution)/shard_map/all_to_all | solution.py:132
  320.4 10.9 %copy-start.3 = (f32[32,4,16,128]{3,2,1,0:T(8,128)}, f32[32,4,16,128]{3,2,1,0:T(8,128)S(1)}, u32[]{:S(2)}) copy-start(f32[32,4,16,128]{3,2,1,0:T(8,128)S(1)} %copy.73) | copy-start | bytes 3145732
  331.3 15.0 %copy-start.1 = (f32[1,32,64,128]{3,2,1,0:T(8,128)}, f32[1,32,64,128]{3,2,1,0:T(8,128)S(1)}, u32[]{:S(2)}) copy-start(f32[1,32,64,128]{3,2,1,0:T(8,128)S(1)} %get-tuple-element.10) | copy-start | bytes 3145732
  331.3 2.6 collective-permute-start.6
  332.6 5.2 collective-permute-start.7
  334.0 11.3 %copy-start.11 = (f32[2,1,64,128]{3,2,1,0:T(8,128)}, f32[2,1,64,128]{3,2,1,0:T(8,128)S(1)}, u32[]{:S(2)}) copy-start(f32[2,1,64,128]{3,2,1,0:T(8,128)S(1)} %collective-permute-done.6) | copy-start | bytes 196612
  337.8 7.5 %copy-start.13 = (f32[2,1,64,128]{3,2,1,0:T(8,128)}, f32[2,1,64,128]{3,2,1,0:T(8,128)S(1)}, u32[]{:S(2)}) copy-start(f32[2,1,64,128]{3,2,1,0:T(8,128)S(1)} %collective-permute-done.7) | copy-start | bytes 196612
  337.9 4.3 collective-permute-start.8
  340.6 4.7 collective-permute-start.9
  342.1 3.2 copy-start.16
  345.3 0.6 copy-start.18
  351.8 9.7 %collective-permute-start.10 = (f32[2,34,66,1]{2,0,3,1:T(2,128)}, f32[2,34,66,1]{2,0,3,1:T(2,128)}, u32[]{:S(2)}, u32[]{:S(2)}) collective-permute-start(f32[2,34,66,1]{2,0,3,1:T(2,128)} %copy.78), channel_id=1, source_target_pairs={{0,1},{1,2},{2,3},{4,5},{5,6},{6,7},{8,9},{9,10},{10,11},{12,13},{... | collective-permute-start | bytes 53864 | tf_op jit(solution)/shard_map/ppermute | solution.py:22
  359.1 5.5 %collective-permute-start.11 = (f32[2,34,66,1]{2,0,3,1:T(2,128)}, f32[2,34,66,1]{2,0,3,1:T(2,128)S(1)}, u32[]{:S(2)}, u32[]{:S(2)}) collective-permute-start(f32[2,34,66,1]{2,0,3,1:T(2,128)} %copy.79), channel_id=1, source_target_pairs={{1,0},{2,1},{3,2},{5,4},{6,5},{7,6},{9,8},{10,9},{11,10},{13,12},{... | collective-permute-start | bytes 53864 | tf_op jit(solution)/shard_map/ppermute | solution.py:24
  361.4 5.6 %copy-start.2 = (f32[1,32,64,128]{3,2,1,0:T(8,128)S(1)}, f32[1,32,64,128]{3,2,1,0:T(8,128)}, u32[]{:S(2)}) copy-start(f32[1,32,64,128]{3,2,1,0:T(8,128)} %copy-done.1) | copy-start | bytes 3145732
  361.4 5.6 %copy-start.12 = (f32[2,1,64,128]{3,2,1,0:T(8,128)S(1)}, f32[2,1,64,128]{3,2,1,0:T(8,128)}, u32[]{:S(2)}) copy-start(f32[2,1,64,128]{3,2,1,0:T(8,128)} %copy-done.11) | copy-start | bytes 196612
  361.4 5.6 %copy-start.14 = (f32[2,1,64,128]{3,2,1,0:T(8,128)S(1)}, f32[2,1,64,128]{3,2,1,0:T(8,128)}, u32[]{:S(2)}) copy-start(f32[2,1,64,128]{3,2,1,0:T(8,128)} %copy-done.13) | copy-start | bytes 196612
  361.4 5.6 %copy-start.17 = (f32[2,34,1,128]{3,2,1,0:T(1,128)S(1)}, f32[2,34,1,128]{3,2,1,0:T(1,128)}, u32[]{:S(2)}) copy-start(f32[2,34,1,128]{3,2,1,0:T(1,128)} %copy-done.16) | copy-start | bytes 104452
  361.4 5.6 %copy-start.19 = (f32[2,34,1,128]{3,2,1,0:T(1,128)S(1)}, f32[2,34,1,128]{3,2,1,0:T(1,128)}, u32[]{:S(2)}) copy-start(f32[2,34,1,128]{3,2,1,0:T(1,128)} %copy-done.18) | copy-start | bytes 104452
  374.3 1.2 copy-start.4
  375.5 11.0 %copy-start.15 = (s32[4096,3]{0,1:T(4,128)S(1)}, s32[4096,3]{0,1:T(4,128)}, u32[]{:S(2)}) copy-start(s32[4096,3]{0,1:T(4,128)} %param.13) | copy-start | bytes 147460
  379.6 7.4 %collective-permute-start.12 = (f32[2,1,64,128]{3,2,1,0:T(8,128)S(1)}, f32[2,1,64,128]{3,2,1,0:T(8,128)S(1)}, u32[]{:S(2)}, u32[]{:S(2)}) collective-permute-start(f32[2,1,64,128]{3,2,1,0:T(8,128)S(1)} %get-tuple-element.33), channel_id=1, source_target_pairs={{0,32},{32,64},{64,96},{96,128},{128,160},{160,192},{192,224},{1,3... | collective-permute-start | bytes 196616 | tf_op jit(solution)/shard_map/ppermute | solution.py:22
  385.2 5.9 %collective-permute-start.13 = (f32[2,1,64,128]{3,2,1,0:T(8,128)S(1)}, f32[2,1,64,128]{3,2,1,0:T(8,128)S(1)}, u32[]{:S(2)}, u32[]{:S(2)}) collective-permute-start(f32[2,1,64,128]{3,2,1,0:T(8,128)S(1)} %get-tuple-element.34), channel_id=1, source_target_pairs={{32,0},{64,32},{96,64},{128,96},{160,128},{192,160},{224,192},{33,... | collective-permute-start | bytes 196616 | tf_op jit(solution)/shard_map/ppermute | solution.py:24
  391.2 8.1 %collective-permute-start.14 = (f32[2,34,1,128]{3,2,1,0:T(1,128)S(1)}, f32[2,34,1,128]{3,2,1,0:T(1,128)S(1)}, u32[]{:S(2)}, u32[]{:S(2)}) collective-permute-start(f32[2,34,1,128]{3,2,1,0:T(1,128)S(1)} %get-tuple-element.27), channel_id=1, source_target_pairs={{0,4},{4,8},{8,12},{12,16},{16,20},{20,24},{24,28},{1,5},{5,9},{9,... | collective-permute-start | bytes 104456 | tf_op jit(solution)/shard_map/ppermute | solution.py:22
  398.0 5.0 collective-permute-start.15
  408.9 10.6 %collective-permute-start.16 = (f32[2,34,66,1]{2,0,3,1:T(2,128)S(1)}, f32[2,34,66,1]{2,0,3,1:T(2,128)S(1)}, u32[]{:S(2)}, u32[]{:S(2)}) collective-permute-start(f32[2,34,66,1]{2,0,3,1:T(2,128)S(1)} %copy.82), channel_id=1, source_target_pairs={{0,1},{1,2},{2,3},{4,5},{5,6},{6,7},{8,9},{9,10},{10,11},{12,13},{... | collective-permute-start | bytes 53864 | tf_op jit(solution)/shard_map/ppermute | solution.py:22
  416.5 5.4 collective-permute-start.17
  437.1 23.0 %copy-start = (f32[32,64,128]{2,1,0:T(8,128)}, f32[32,64,128]{2,1,0:T(8,128)S(1)}, u32[]{:S(2)}) copy-start(f32[32,64,128]{2,1,0:T(8,128)S(1)} %get-tuple-element.5) | copy-start | bytes 3145732
  437.1 104.4 %copy-start.21 = (f32[4096]{0:T(1024)S(1)}, f32[4096]{0:T(1024)}, u32[]{:S(2)}) copy-start(f32[4096]{0:T(1024)} %param.14) | copy-start | bytes 49156
  541.6 1.3 copy-start.20
where the time goes:
time: 555 us; the launch traced here: 544 us
  blocking collectives  179 us (32%)
  local copies, waits for them, and re-layouts  131 us (24%)
  other arithmetic  71.6 us (13%)
  starting transfers between devices  60.1 us (11%)
  matrix products  55 us (10%)
  waiting for transfers between devices  41.6 us (7%)
  between operations  6.4 us (1%)
    psum x1, blocking collectives, body(): lax.psum(detector_inside_subdomain, ('gx', 'gy', 'gz'))  81.4 us
    all_to_all x1, blocking collectives, body(): lax.all_to_all(jnp.stack([real, imag]), 'gx', split_axis=3, concat_axis=2...  58.6 us
    all_to_all x1, blocking collectives, body(): lax.all_to_all(stacked, ('gy', 'gz'), split_axis=2, concat_axis=1, tiled=...  38.5 us
    ppermute x9, starting transfers between devices, padded_2(): lax.ppermute(tail, axis, [(i, (i + 1) % count) for i in range(ends)])  37.1 us
    unnamed x52, local copies, waits for them, and re-layouts  31.8 us
    unnamed x6, matrix products  31.5 us
    ppermute x9, waiting for transfers between devices, padded_2(): lax.ppermute(head, axis, [((i + 1) % count, i) for i in range(ends)])  23.1 us
    gather x1, local copies, waits for them, and re-layouts, body(): ending_kelvin_array.reshape(-1)[flattened_cell_offset]  23 us
  transfers between devices with their start and end apart: 20, of which 10 were waited for; matrix products, arithmetic and copies ran while one was open for 6% of the time, Pallas kernels for 0%

commit v1 on v0

v1 whole, which is shorter than its diff:
```python
import functools
import math

import jax
import jax.numpy as jnp
import ml_dtypes
import numpy as np
from jax import lax
from jax.experimental import pallas as pl
from jax.experimental.pallas import tpu as pltpu
from jax.sharding import PartitionSpec as P

MESH_EXTENT_EAST = 256
MESH_EXTENT_NORTH = 512
MESH_EXTENT_UPWARD = 512
STEPS = 3
S = 4096
CHUNKS = 4
MESH = pl.DeviceIdType.MESH
F32 = jnp.float32
BF16 = jnp.bfloat16
NT = (((1,), (1,)), ((), ()))


def spectrum(length):
    wave = np.arange(length)
    signed = np.where(wave < length // 2, wave, wave - length).astype(np.float64)
    shape = 1.0 / np.sqrt(1.0 + (signed / 8.0) ** 2)
    return shape / np.sqrt(np.sum(shape * shape))


def waves(places, numbers, length):
    angle = (places[:, None] * numbers[None, :] % length) * (2.0 * math.pi / length)
    scale = spectrum(length)[numbers][None, :]
    return np.cos(angle) * scale, np.sin(angle) * scale


def halves(table):
    high = table.astype(np.float32).astype(ml_dtypes.bfloat16)
    low = (table - high.astype(np.float64)).astype(np.float32).astype(ml_dtypes.bfloat16)
    return high, low


def tables(gx, gy, gz, nx, ny, nz):
    sub = nz // (gy * gz)
    part = sub // CHUNKS
    stacks = []
    for chunk in range(CHUNKS):
        places = np.concatenate(
            [
                z * (nz // gz) + y * sub + chunk * part + np.arange(part)
                for y in range(gy)
                for z in range(gz)
            ]
        )
        cosine, sine = waves(places, np.arange(nz), nz)
        stacks.append(np.concatenate(halves(np.concatenate([cosine, sine]))))
    depth = np.stack(stacks)
    cosine, sine = waves(np.arange(nx), np.arange(nx), nx)
    first = np.concatenate(halves(np.concatenate([cosine, sine])))
    width = ny // gx
    blocks = []
    for block in range(gx):
        cosine, sine = waves(np.arange(ny), block * width + np.arange(width), ny)
        blocks += [cosine.T, -sine.T]
    second = np.stack(halves(np.concatenate(blocks)))
    return depth, first, second


def split(values):
    high = values.astype(BF16)
    return high, (values - high.astype(F32)).astype(BF16)


def kernel(
    dims,
    beta,
    sensor_x,
    sensor_y,
    sensor_z,
    cost,
    inc,
    ren,
    w1_hbm,
    w2_hbm,
    w3_hbm,
    rho0,
    heat0,
    recorded,
    thr_out,
    rho_out,
    heat_out,
    model_out,
    odds_out,
    inc_v,
    ren_v,
    b_high,
    b_low,
    w1,
    w2,
    w3,
    send1,
    got1,
    send2,
    got2,
    send3,
    got3,
    thr,
    state,
    hx_send,
    hx_got,
    hy_send,
    hy_got,
    hz_send,
    hz_got,
    gathered,
    red_send,
    red_a,
    red_mid,
    red_b,
    red_fin,
    red_c,
    load_sem,
    out_sem,
    s1_sem,
    r1_sem,
    s2_sem,
    r2_sem,
    s3_sem,
    r3_sem,
    hs_sem,
    hr_sem,
    rs_sem,
    rr_sem,
):
    gx, gy, gz, nx, ny, nz = dims
    nd = gy * gz
    sub = nz // nd
    part = sub // CHUNKS
    bx, by, bz = nx // gx, ny // gy, nz // gz
    half = bx // 2
    kx_own = nx // nd
    ix, iy, iz = lax.axis_index("gx"), lax.axis_index("gy"), lax.axis_index("gz")
    me = iy * gz + iz

    def plane_device(k):
        other = lax.rem(me + k, nd)
        return other, (ix, other // gz, lax.rem(other, gz))

    def line_device(k):
        other = lax.rem(ix + k, gx)
        return other, (other, iy, iz)

    def row_device(k):
        other = lax.rem(iy + k, gy)
        return other, (ix, other, iz)

    loads = [
        pltpu.make_async_copy(inc, inc_v, load_sem.at[0]),
        pltpu.make_async_copy(ren, ren_v, load_sem.at[1]),
        pltpu.make_async_copy(w1_hbm, w1, load_sem.at[2]),
        pltpu.make_async_copy(heat0, state.at[0, 0, pl.ds(1, bx), pl.ds(8, by), :], load_sem.at[3]),
        pltpu.make_async_copy(rho0, state.at[0, 1, pl.ds(1, bx), pl.ds(8, by), :], load_sem.at[4]),
        pltpu.make_async_copy(w2_hbm, w2, load_sem.at[5]),
        pltpu.make_async_copy(w3_hbm, w3, load_sem.at[6]),
    ]
    for load in loads:
        load.start()

    barrier = pltpu.get_barrier_semaphore()

    def greet_plane(k, carry):
        pl.semaphore_signal(barrier, inc=1, device_id=plane_device(k)[1], device_id_type=MESH)
        return carry

    def greet_line(k, carry):
        pl.semaphore_signal(barrier, inc=1, device_id=line_device(k)[1], device_id_type=MESH)
        return carry

    lax.fori_loop(1, nd, greet_plane, 0)
    lax.fori_loop(1, gx, greet_line, 0)

    lane = lax.broadcasted_iota(jnp.int32, (1, 128), 1)
    sign = jnp.where(lane < 64, -1.0, 1.0).astype(F32)
    first_half = lane < 64

    sides = [("x", ix, gx, 0), ("y", iy, gy, 1), ("z", iz, gz, 2)]
    got = {"x": hx_got, "y": hy_got, "z": hz_got}
    sent = {"x": hx_send, "y": hy_send, "z": hz_send}
    outside = jnp.where(lane < bx, 1.25, 0.0).astype(F32)
    for name, place, count, number in sides:
        for end in range(2):
            edge = place == (0 if end == 0 else count - 1)

            @pl.when(edge)
            def _(name=name, end=end):
                for step in range(STEPS):
                    if name == "z":
                        hz_got[step, end] = jnp.broadcast_to(outside, hz_got.shape[2:])
                    else:
                        ref = got[name]
                        ref[step, end, 0] = jnp.full(ref.shape[3:], 1.25, F32)
                        ref[step, end, 1] = jnp.zeros(ref.shape[3:], F32)

    loads[0].wait()
    loads[1].wait()
    weight = jnp.full((1, 128), beta[0], F32)
    keep = jnp.sqrt(1.0 - weight * weight)[:, :1]
    fresh = weight[:, :1]

    def mix(k, carry):
        for part_of in range(2):
            mixed = keep * inc_v[part_of, k] + fresh * ren_v[part_of, k]
            high, low = split(mixed)
            rows = pl.ds(pl.multiple_of(k * 128 + part_of * 64, 64), 64)
            b_high[rows, :] = high
            b_low[rows, :] = low
        return carry

    lax.fori_loop(0, kx_own, mix, 0)
    loads[2].wait()
    pl.semaphore_wait(barrier, nd + gx - 2)

    rows1 = nd * part

    def stage1(c):
        flat = send1.at[c].reshape(rows1 * kx_own, 128)
        for q in range(kx_own // 2):
            right = pl.ds(q * 256, 256)
            top = lax.dot_general(w1[c], b_high[right, :], NT, preferred_element_type=F32)
            low = lax.dot_general(
                w1[c, pl.ds(0, 2 * rows1), :], b_low[right, :], NT, preferred_element_type=F32
            )
            total = top[: 2 * rows1] + top[2 * rows1 :] + low
            for side in range(2):
                cut = slice(side * 128, side * 128 + 128)
                cosines = total[:rows1, cut]
                sines = total[rows1:, cut]
                flat[pl.ds(2 * q + side, rows1, stride=kx_own), :] = cosines + sign * pltpu.roll(
                    sines, 64, 1
                )

        pltpu.make_async_copy(
            send1.at[c, pl.ds(me * part, part)],
            got1.at[c, :, pl.ds(pl.multiple_of(me * kx_own, kx_own), kx_own), :],
            r1_sem.at[c],
        ).start()

        def push(k, carry):
            other, device = plane_device(k)
            pltpu.make_async_remote_copy(
                src_ref=send1.at[c, pl.ds(other * part, part)],
                dst_ref=got1.at[c, :, pl.ds(pl.multiple_of(me * kx_own, kx_own), kx_own), :],
                send_sem=s1_sem.at[c],
                recv_sem=r1_sem.at[c],
                device_id=device,
                device_id_type=MESH,
            ).start()
            return carry

        lax.fori_loop(1, nd, push, 0)

    def stage2(c):
        pltpu.make_async_copy(got1.at[c], got1.at[c], r1_sem.at[c]).wait()

        def pair(p, carry):
            values = jnp.concatenate([got1[c, 2 * p], got1[c, 2 * p + 1]], axis=1)
            high, low = split(values)
            top = jnp.dot(w2[...], high, preferred_element_type=F32)
            bottom = jnp.dot(w2[pl.ds(0, 2 * nx), :], low, preferred_element_type=F32)
            total = top[: 2 * nx] + top[2 * nx :] + bottom
            for side in range(2):
                cut = slice(side * 128, side * 128 + 128)
                send2[c, 2 * p + side] = total[:nx, cut] + sign * pltpu.roll(total[nx:, cut], 64, 1)
            return carry

        lax.fori_loop(0, part // 2, pair, 0)
        pltpu.make_async_copy(
            send2.at[c, :, pl.ds(pl.multiple_of(ix * bx, bx), bx), :], got2.at[c, ix], r2_sem.at[c]
        ).start()

        def push(k, carry):
            other, device = line_device(k)
            pltpu.make_async_remote_copy(
                src_ref=send2.at[c, :, pl.ds(pl.multiple_of(other * bx, bx), bx), :],
                dst_ref=got2.at[c, ix],
                send_sem=s2_sem.at[c],
                recv_sem=r2_sem.at[c],
                device_id=device,
                device_id_type=MESH,
            ).start()
            return carry

        lax.fori_loop(1, gx, push, 0)

    def stage3(c):
        pltpu.make_async_copy(got2.at[c], got2.at[c], r2_sem.at[c]).wait()
        values = jnp.concatenate(
            [got2[c, g].reshape(part * bx, 128) for g in range(gx)], axis=1
        )
        high, low = split(values)
        rows = part * bx
        both = jnp.concatenate([high, low], axis=0)
        for t in range(ny // 256):
            columns = pl.ds(t * 256, 256)
            top = jnp.dot(both, w3[0, :, columns], preferred_element_type=F32)
            field = (
                top[:rows]
                + top[rows:]
                + jnp.dot(high, w3[1, :, columns], preferred_element_type=F32)
            )
            energy = 2.0 + 0.6 * jnp.tanh(field)
            for side in range(2):
                tile = energy[:, side * 128 : side * 128 + 128].reshape(part, 2, half, 128)
                near, far = tile[:, 0], tile[:, 1]
                near = near.reshape(part * half, 128)
                far = far.reshape(part * half, 128)
                j = 4 * t + 2 * side
                send3[c, j] = jnp.where(first_half, near, pltpu.roll(far, 64, 1))
                send3[c, j + 1] = jnp.where(first_half, pltpu.roll(near, 64, 1), far)
        target = got3.at[
            pl.ds(pl.multiple_of((iy * sub + c * part) * half, part * half), part * half), :
        ]
        pltpu.make_async_copy(send3.at[c, iy], target, r3_sem.at[0]).start()

        def push(k, carry):
            other, device = row_device(k)
            pltpu.make_async_remote_copy(
                src_ref=send3.at[c, other],
                dst_ref=target,
                send_sem=s3_sem.at[0],
                recv_sem=r3_sem.at[0],
                device_id=device,
                device_id_type=MESH,
            ).start()
            return carry

        lax.fori_loop(1, gy, push, 0)

    def exchange(step, now):
        def pack(x, carry):
            for f in range(2):
                plane = state[now, f, x + 1, pl.ds(8, by), :]
                hy_send[step, 0, f, pl.ds(x, 1), :] = plane[:1]
                hy_send[step, 1, f, pl.ds(x, 1), :] = plane[by - 1 :]
                here = lane == f * bx + x
                hz_send[step, 0] = jnp.where(
                    here, pltpu.roll(plane, f * bx + x, 1), hz_send[step, 0]
                )
                hz_send[step, 1] = jnp.where(
                    here, pltpu.roll(plane, f * bx + x + 1, 1), hz_send[step, 1]
                )
            return carry

        hz_send[step] = jnp.zeros(hz_send.shape[1:], F32)
        lax.fori_loop(0, bx, pack, 0)
        for f in range(2):
            hx_send[step, 0, f] = state[now, f, 1, pl.ds(8, by), :]
            hx_send[step, 1, f] = state[now, f, bx, pl.ds(8, by), :]
        for name, place, count, number in sides:
            for end in range(2):
                move = -1 if end == 0 else 1
                inner = place > 0 if end == 0 else place < count - 1
                device = [ix, iy, iz]
                device[number] = device[number] + move

                @pl.when(inner)
                def _(name=name, end=end, device=tuple(device), number=number):
                    pltpu.make_async_remote_copy(
                        src_ref=sent[name].at[step, end],
                        dst_ref=got[name].at[step, 1 - end],
                        send_sem=hs_sem.at[step, number, end],
                        recv_sem=hr_sem.at[step, number, 1 - end],
                        device_id=device,
                        device_id_type=MESH,
                    ).start()

    def receive(step, now):
        for name, place, count, number in sides:
            for end in range(2):
                inner = place > 0 if end == 0 else place < count - 1

                @pl.when(inner)
                def _(name=name, end=end, number=number):
                    ref = got[name].at[step, end]
                    pltpu.make_async_copy(ref, ref, hr_sem.at[step, number, end]).wait()

        for f in range(2):
            state[now, f, 0, pl.ds(8, by), :] = hx_got[step, 0, f]
            state[now, f, bx + 1, pl.ds(8, by), :] = hx_got[step, 1, f]

        def unpack(x, carry):
            for f in range(2):
                state[now, f, x + 1, pl.ds(7, 1), :] = hy_got[step, 0, f, pl.ds(x, 1), :]
                state[now, f, x + 1, pl.ds(8 + by, 1), :] = hy_got[step, 1, f, pl.ds(x, 1), :]
            return carry

        lax.fori_loop(0, bx, unpack, 0)

    def advance(step, now):
        def plane(x, carry):
            def at(f, dx, dy):
                return state[now, f, x + 1 + dx, pl.ds(8 + dy, by), :]

            heat, rho = at(0, 0, 0), at(1, 0, 0)
            cond = rho * rho
            flux = jnp.zeros_like(heat)
            around = [
                (at(0, 1, 0), at(1, 1, 0)),
                (at(0, -1, 0), at(1, -1, 0)),
                (at(0, 0, 1), at(1, 0, 1)),
                (at(0, 0, -1), at(1, 0, -1)),
            ]
            for end in range(2):
                packed = hz_got[step, end]
                edge = 0 if end == 0 else 127
                turn = 1 if end == 0 else 127
                pair = []
                for f, values in ((0, heat), (1, rho)):
                    shift = lax.rem(edge + 256 - f * bx - x, 128)
                    pair.append(
                        jnp.where(
                            lane == edge, pltpu.roll(packed, shift, 1), pltpu.roll(values, turn, 1)
                        )
                    )
                around.append(tuple(pair))
            for heat_side, rho_side in around:
                flux = flux + (cond + rho_side * rho_side) * (heat_side - heat)
            growth = jnp.exp(-thr[x] / heat) * (1.0 - rho)
            state[1 - now, 0, x + 1, pl.ds(8, by), :] = heat + 0.16 * (0.5 * flux + 3.0 * growth)
            state[1 - now, 1, x + 1, pl.ds(8, by), :] = rho + 0.64 * growth
            return carry

        lax.fori_loop(0, bx, plane, 0)

    def pipeline(i, carry):
        @pl.when(i < CHUNKS)
        def _():
            stage1(i)

        @pl.when(i == 0)
        def _():
            for load in loads[3:]:
                load.wait()
            exchange(0, 0)

        @pl.when((i >= 1) & (i <= CHUNKS))
        def _():
            stage2(i - 1)

        @pl.when(i >= 2)
        def _():
            stage3(i - 2)

        return carry

    lax.fori_loop(0, CHUNKS + 2, pipeline, 0)

    pltpu.make_async_copy(got3, got3, r3_sem.at[0]).wait()
    for x in range(half):
        turned = got3[pl.ds(x, bz, stride=half), :].T
        thr[x] = turned[:by]
        thr[half + x] = turned[by:]
    thr_copy = pltpu.make_async_copy(thr, thr_out, out_sem.at[0])
    thr_copy.start()

    for step in range(STEPS):
        now = step % 2
        if step:
            exchange(step, now)
        receive(step, now)
        advance(step, now)
    last = STEPS % 2
    heat_copy = pltpu.make_async_copy(
        state.at[last, 0, pl.ds(1, bx), pl.ds(8, by), :], heat_out, out_sem.at[1]
    )
    rho_copy = pltpu.make_async_copy(
        state.at[last, 1, pl.ds(1, bx), pl.ds(8, by), :], rho_out, out_sem.at[2]
    )
    heat_copy.start()
    rho_copy.start()

    def look(g, carry):
        rows = []
        for k in range(8):
            s = g * 8 + k
            row = state[last, 0, sensor_x[s], pl.ds(sensor_y[s], 1), :]
            rows.append(jnp.where(lane == sensor_z[s], row, 0.0))
        gathered[pl.ds(pl.multiple_of(g * 8, 8), 8), :] = jnp.concatenate(rows, axis=0)
        return carry

    lax.fori_loop(0, S // 8, look, 0)
    ones = jnp.ones((8, 128), F32)
    per = S // 128 // gx
    for block in range(gx):
        red_send[block] = jnp.zeros((8, 128), F32)
        for k in range(per):
            values = gathered[pl.ds((block * per + k) * 128, 128), :]
            sums = lax.dot_general(
                ones, values, NT, precision=lax.Precision.HIGHEST, preferred_element_type=F32
            )
            red_send[block, pl.ds(k, 1), :] = sums[:1]

    pltpu.make_async_copy(red_send.at[ix], red_a.at[ix], rr_sem.at[0]).start()

    def push_a(k, carry):
        other, device = line_device(k)
        pltpu.make_async_remote_copy(
            src_ref=red_send.at[other],
            dst_ref=red_a.at[ix],
            send_sem=rs_sem.at[0],
            recv_sem=rr_sem.at[0],
            device_id=device,
            device_id_type=MESH,
        ).start()
        return carry

    lax.fori_loop(1, gx, push_a, 0)
    pltpu.make_async_copy(red_a, red_a, rr_sem.at[0]).wait()
    red_mid[...] = jnp.sum(red_a[...], axis=0)
    pltpu.make_async_copy(red_mid, red_b.at[me], rr_sem.at[1]).start()

    def push_b(k, carry):
        other, device = plane_device(k)
        pltpu.make_async_remote_copy(
            src_ref=red_mid,
            dst_ref=red_b.at[me],
            send_sem=rs_sem.at[1],
            recv_sem=rr_sem.at[1],
            device_id=device,
            device_id_type=MESH,
        ).start()
        return carry

    lax.fori_loop(1, nd, push_b, 0)
    pltpu.make_async_copy(red_b, red_b, rr_sem.at[1]).wait()
    red_fin[...] = jnp.sum(red_b[...], axis=0)
    pltpu.make_async_copy(red_fin, red_c.at[ix], rr_sem.at[2]).start()

    def push_c(k, carry):
        other, device = line_device(k)
        pltpu.make_async_remote_copy(
            src_ref=red_fin,
            dst_ref=red_c.at[ix],
            send_sem=rs_sem.at[2],
            recv_sem=rr_sem.at[2],
            device_id=device,
            device_id_type=MESH,
        ).start()
        return carry

    lax.fori_loop(1, gx, push_c, 0)
    pltpu.make_async_copy(red_c, red_c, rr_sem.at[2]).wait()
    misfit = jnp.zeros((per, 128), F32)
    for block in range(gx):
        values = red_c[block, pl.ds(0, per), :]
        model_out[pl.ds(block * per, per), :] = values
        gap = (values - recorded[pl.ds(block * per, per), :]) / 0.2
        misfit = misfit + gap * gap
    odds_out[0] = cost[0] - 0.5 * (jnp.sum(misfit) / S)

    def drain(ref, sem):
        pltpu.make_async_copy(ref, ref, sem).wait()

    def drain_chunk(c, carry):
        drain(send1.at[c, pl.ds(0, (nd - 1) * part)], s1_sem.at[c])
        drain(send2.at[c, :, pl.ds(0, nx - bx), :], s2_sem.at[c])
        return carry

    lax.fori_loop(0, CHUNKS, drain_chunk, 0)
    drain(send3.at[:, pl.ds(0, gy - 1)], s3_sem.at[0])
    for name, place, count, number in sides:
        for end in range(2):
            inner = place > 0 if end == 0 else place < count - 1

            @pl.when(inner)
            def _(name=name, end=end, number=number):
                for step in range(STEPS):
                    drain(sent[name].at[step, end], hs_sem.at[step, number, end])

    drain(red_a.at[pl.ds(0, gx - 1)], rs_sem.at[0])
    drain(red_b.at[pl.ds(0, nd - 1)], rs_sem.at[1])
    drain(red_c.at[pl.ds(0, gx - 1)], rs_sem.at[2])
    thr_copy.wait()
    heat_copy.wait()
    rho_copy.wait()


def solution(mesh):
    gx, gy, gz = (mesh.shape[name] for name in ("gx", "gy", "gz"))
    nx, ny, nz = MESH_EXTENT_EAST, MESH_EXTENT_NORTH, MESH_EXTENT_UPWARD
    depth, first, second = tables(gx, gy, gz, nx, ny, nz)
    nd = gy * gz
    sub = nz // nd
    part = sub // CHUNKS
    bx, by, bz = nx // gx, ny // gy, nz // gz
    kx_own, ky_own = nx // nd, ny // gx

    def body(incumbent, renewed, beta, rho, heat, place, recorded, cost):
        local_x = place[:, 0] - lax.axis_index("gx") * bx
        local_y = place[:, 1] - lax.axis_index("gy") * by
        local_z = place[:, 2] - lax.axis_index("gz") * bz
        own = (
            (local_x >= 0)
            & (local_x < bx)
            & (local_y >= 0)
            & (local_y < by)
            & (local_z >= 0)
            & (local_z < bz)
        )
        sensor_x = jnp.clip(local_x, 0, bx - 1) + 1
        sensor_y = jnp.clip(local_y, 0, by - 1) + 8
        sensor_z = jnp.where(own, local_z, -1)
        smem = pl.BlockSpec(memory_space=pltpu.SMEM)
        hbm = pl.BlockSpec(memory_space=pl.ANY)
        vmem = pl.BlockSpec(memory_space=pltpu.VMEM)
        dma = pltpu.SemaphoreType.DMA
        block = jax.ShapeDtypeStruct((bx, by, bz), F32)
        outs = pl.pallas_call(
            functools.partial(kernel, (gx, gy, gz, nx, ny, nz)),
            out_shape=(
                block,
                block,
                block,
                jax.ShapeDtypeStruct((S // 128, 128), F32),
                jax.ShapeDtypeStruct((1,), F32),
            ),
            in_specs=[smem] * 5 + [hbm] * 7 + [vmem],
            out_specs=(hbm, hbm, hbm, vmem, smem),
            scratch_shapes=[
                pltpu.VMEM((2, kx_own, ky_own, nz), F32),
                pltpu.VMEM((2, kx_own, ky_own, nz), F32),
                pltpu.VMEM((kx_own * 2 * ky_own, nz), BF16),
                pltpu.VMEM((kx_own * 2 * ky_own, nz), BF16),
                pltpu.VMEM(depth.shape, BF16),
                pltpu.VMEM(first.shape, BF16),
                pltpu.VMEM(second.shape, BF16),
                pltpu.VMEM((CHUNKS, nd * part, kx_own, 128), F32),
                pltpu.VMEM((CHUNKS, part, nx, 128), F32),
                pltpu.VMEM((CHUNKS, part, nx, 128), F32),
                pltpu.VMEM((CHUNKS, gx, part, bx, 128), F32),
                pltpu.VMEM((CHUNKS, gy, part * bx // 2, 128), F32),
                pltpu.VMEM((bz * bx // 2, 128), F32),
                pltpu.VMEM((bx, by, bz), F32),
                pltpu.VMEM((2, 2, bx + 2, by + 16, bz), F32),
                pltpu.VMEM((STEPS, 2, 2, by, bz), F32),
                pltpu.VMEM((STEPS, 2, 2, by, bz), F32),
                pltpu.VMEM((STEPS, 2, 2, bx, bz), F32),
                pltpu.VMEM((STEPS, 2, 2, bx, bz), F32),
                pltpu.VMEM((STEPS, 2, by, bz), F32),
                pltpu.VMEM((STEPS, 2, by, bz), F32),
                pltpu.VMEM((S, 128), F32),
                pltpu.VMEM((gx, 8, 128), F32),
                pltpu.VMEM((gx, 8, 128), F32),
                pltpu.VMEM((8, 128), F32),
                pltpu.VMEM((nd, 8, 128), F32),
                pltpu.VMEM((8, 128), F32),
                pltpu.VMEM((gx, 8, 128), F32),
                dma((7,)),
                dma((3,)),
                dma((CHUNKS,)),
                dma((CHUNKS,)),
                dma((CHUNKS,)),
                dma((CHUNKS,)),
                dma((1,)),
                dma((1,)),
                dma((STEPS, 3, 2)),
                dma((STEPS, 3, 2)),
                dma((3,)),
                dma((3,)),
            ],
            compiler_params=pltpu.CompilerParams(
                collective_id=0, has_side_effects=True, vmem_limit_bytes=56 * 1024 * 1024
            ),
            cost_estimate=pl.CostEstimate(
                flops=7_000_000_000, bytes_accessed=16_000_000, transcendentals=1_000_000
            ),
        )(
            beta,
            sensor_x,
            sensor_y,
            sensor_z,
            cost,
            incumbent,
            renewed,
            jnp.asarray(depth),
            jnp.asarray(first),
            jnp.asarray(second),
            rho,
            heat,
            recorded.reshape(S // 128, 128),
        )
        energy, density, kelvin, model, odds = outs
        return energy, density, kelvin, model.reshape(S), odds

    return jax.shard_map(
        body,
        mesh=mesh,
        in_specs=(
            P(None, ("gy", "gz"), "gx", None),
            P(None, ("gy", "gz"), "gx", None),
            P(),
            P("gx", "gy", "gz"),
            P("gx", "gy", "gz"),
            P(),
            P(),
            P(),
        ),
        out_specs=(P("gx", "gy", "gz"), P("gx", "gy", "gz"), P("gx", "gy", "gz"), P(), P()),
        check_vma=False,
    )
```

time: 555 us -> 158 us (0.28); the launches traced: 544 us -> 158 us
  blocking collectives: 179 us -> 0 us
  Pallas kernels: 0 us -> 146 us
  local copies, waits for them, and re-layouts: 131 us -> 5.01 us
  other arithmetic: 71.6 us -> 3.27 us
  starting transfers between devices: 60.1 us -> 0 us
  matrix products: 55 us -> 0 us
  waiting for transfers between devices: 41.6 us -> 0 us
    pallas_call x0 -> x1, Pallas kernels: none -> 146 us  [body(): pl.pallas_call(functools.partial(kernel, (gx, gy, gz, nx, ny, nz)), out_s...]
    all_to_all x2 -> x0, blocking collectives: 97.1 us -> none  [the longest x1 58.6 us: body(): lax.all_to_all(jnp.stack([real, imag]), 'gx', split_axis=3, concat_axis=2...]
    psum x1 -> x0, blocking collectives: 81.4 us -> none  [body(): lax.psum(detector_inside_subdomain, ('gx', 'gy', 'gz'))]
    ppermute x18 -> x0, starting transfers between devices: 51.5 us -> none  [the longest x9 37.1 us: padded_2(): lax.ppermute(tail, axis, [(i, (i + 1) % count) for i in range(ends)])]
    ppermute x18 -> x0, waiting for transfers between devices: 40.3 us -> none  [the longest x9 23.1 us: padded_2(): lax.ppermute(head, axis, [((i + 1) % count, i) for i in range(ends)])]
    unnamed x6 -> x0, matrix products: 31.5 us -> none
    slice x13 -> x0, local copies, waits for them, and re-layouts: 27 us -> none  [the longest x6 16.6 us: padded_2(): lax.slice_in_dim(cells, cells.shape[dim] - width, cells.shape[dim], axis=...]
    unnamed x52 -> x10, local copies, waits for them, and re-layouts: 31.8 us -> 5.01 us
  transfers between devices with their start and end apart: 20 -> 0, of which waited for: 10 -> 0; matrix products, arithmetic and copies ran while one was open for 6% -> 0% of each run, Pallas kernels for 0% -> 0%
where the time goes in v1:
time: 158 us
  Pallas kernels  146 us (92%)
  local copies, waits for them, and re-layouts  5.01 us (3%)
  between operations  3.64 us (2%)
  other arithmetic  3.27 us (2%)
    pallas_call x1, Pallas kernels, body(): pl.pallas_call(functools.partial(kernel, (gx, gy, gz, nx, ny, nz)), out_s...  146 us
    unnamed x10, local copies, waits for them, and re-layouts  5.01 us

profile of v1, /device:TPU:1, one launch (start us, length us, event | category | flops | bytes accessed | tf_op | source)
XLA Modules:
  0.0 157.8 jit_solution(571916920334798092)
XLA Ops:
  1.9 1.0 and_reduce_fusion
  2.9 1.6 %slice_subtract_fusion = (s32[4096,1]{0,1:T(1,128)S(1)}, s32[4096,1]{0,1:T(1,128)}, s32[4096,1]{0,1:T(1,128)}) fusion(s32[4096,3]{0,1:T(4,128)} %param.16, s32[]{:T(128)S(6)} %mul.11, s32[]{:T(128)S(6)} %mul.9, s32[]{:T(128)S(6)} %mul.10), kind=kLoop, calls=%fused_computation.1 | loop fusion | flops 28672 | bytes 98316 | tf_op jit(solution)/shard_map/sub | solution.py:602
  4.6 0.6 and_select_fusion.sensor_z
  5.2 145.9 %shard_map.146 = (f32[32,64,128]{2,1,0:T(8,128)}, f32[32,64,128]{2,1,0:T(8,128)}, f32[32,64,128]{2,1,0:T(8,128)}, f32[32,128]{1,0:T(8,128)}, f32[1]{0:T(128)}) custom-call(f32[1]{0:T(128)S(6)} %copy.21.beta, s32[4096]{0:T(1024)} %bitcast.6, s32[4096]{0:T(1024)} %bitcast.7, s32[4096]{0:T(1024)} %and_select_fusion.sensor_z, f32[1]{0:T(128)S(6)} %copy.22.cost, ...), custom_call_target="tpu_custom_call" | custom-call | flops 7000000000 | bytes 16000000 | tf_op jit(solution)/shard_map/pallas_call | solution.py:619
  151.1 0.0 copy-start.1
  151.1 0.0 copy-start
  151.2 2.5 %copy.23 = f32[32,64,128]{2,1,0:T(8,128)} copy(f32[32,64,128]{2,1,0:T(8,128)} %get-tuple-element.23) | data formatting | bytes 2097152
  153.6 0.0 copy-done.1
  153.6 0.0 copy-start.2
  153.6 1.0 copy.24
  154.6 0.0 copy-done
  154.6 1.0 copy.25
  155.6 0.0 copy-done.2
  155.6 0.6 copy.26
Async XLA Ops:
  151.1 2.5 %copy-start.1 = (f32[32,64,128]{2,1,0:T(8,128)S(1)}, f32[32,64,128]{2,1,0:T(8,128)}, u32[]{:S(2)}) copy-start(f32[32,64,128]{2,1,0:T(8,128)} %get-tuple-element.24) | copy-start | bytes 3145732
  151.1 3.4 %copy-start = (f32[32,64,128]{2,1,0:T(8,128)S(1)}, f32[32,64,128]{2,1,0:T(8,128)}, u32[]{:S(2)}) copy-start(f32[32,64,128]{2,1,0:T(8,128)} %get-tuple-element.25) | copy-start | bytes 3145732
  153.6 1.9 %copy-start.2 = (f32[32,128]{1,0:T(8,128)S(1)}, f32[32,128]{1,0:T(8,128)}, u32[]{:S(2)}) copy-start(f32[32,128]{1,0:T(8,128)} %get-tuple-element.13) | copy-start | bytes 49156

commit v2 on v1

v2 whole, which is shorter than its diff:
```python
import functools
import math

import jax
import jax.numpy as jnp
import ml_dtypes
import numpy as np
from jax import lax
from jax.experimental import pallas as pl
from jax.experimental.pallas import tpu as pltpu
from jax.sharding import PartitionSpec as P

MESH_EXTENT_EAST = 256
MESH_EXTENT_NORTH = 512
MESH_EXTENT_UPWARD = 512
STEPS = 3
S = 4096
CHUNKS = 8
LAG = 3
GROUPS = 4
SLOTS = 8
ABL = set()
MESH = pl.DeviceIdType.MESH
F32 = jnp.float32
BF16 = jnp.bfloat16
NT = (((1,), (1,)), ((), ()))


def spectrum(length):
    wave = np.arange(length)
    signed = np.where(wave < length // 2, wave, wave - length).astype(np.float64)
    shape = 1.0 / np.sqrt(1.0 + (signed / 8.0) ** 2)
    return shape / np.sqrt(np.sum(shape * shape))


def waves(places, numbers, length):
    angle = (places[:, None] * numbers[None, :] % length) * (2.0 * math.pi / length)
    scale = spectrum(length)[numbers][None, :]
    return np.cos(angle) * scale, np.sin(angle) * scale


def halves(table):
    high = table.astype(np.float32).astype(ml_dtypes.bfloat16)
    low = (table - high.astype(np.float64)).astype(np.float32).astype(ml_dtypes.bfloat16)
    return high, low


def tables(gx, gy, gz, nx, ny, nz):
    sub = nz // (gy * gz)
    part = sub // CHUNKS
    stacks = []
    for chunk in range(CHUNKS):
        places = np.concatenate(
            [
                z * (nz // gz) + y * sub + chunk * part + np.arange(part)
                for y in range(gy)
                for z in range(gz)
            ]
        )
        cosine, sine = waves(places, np.arange(nz), nz)
        stacks.append(np.concatenate(halves(np.concatenate([cosine, sine]))))
    depth = np.stack(stacks)
    cosine, sine = waves(np.arange(nx), np.arange(nx), nx)
    first = np.concatenate(halves(np.concatenate([cosine, sine])))
    width = ny // gx
    blocks = []
    for block in range(gx):
        cosine, sine = waves(np.arange(ny), block * width + np.arange(width), ny)
        blocks += [cosine.T, -sine.T]
    second = np.stack(halves(np.concatenate(blocks)))
    return depth, first, second


def split(values):
    high = values.astype(BF16)
    return high, (values - high.astype(F32)).astype(BF16)


PLANE_ORDER = [
    (dx, dy, dc)
    for dx, dy in [
        (2, 2), (1, 0), (0, 1), (3, 0), (0, 3), (2, 1), (1, 2), (2, 3),
        (3, 2), (1, 1), (3, 3), (2, 0), (0, 2), (1, 3), (3, 1), (0, 0),
    ]
    for dc in range(2)
    if (dx, dy, dc) != (0, 0, 0)
]
LINE_ORDER = [4, 3, -3, 2, -2, 1, -1]
ROW_ORDER = [(2, 1), (1, 0), (3, 1), (2, 0), (1, 1), (3, 0), (0, 1)]


def places(gx, gy, gz):
    ix, iy, iz = lax.axis_index("gx"), lax.axis_index("gy"), lax.axis_index("gz")
    nx_ring = gy // 2
    x, y_high = lax.rem(iy, nx_ring), iy // nx_ring
    y, core = y_high * (gz // 2) + iz // 2, lax.rem(iz, 2)
    turn = 1 - 2 * core

    def plane(offset):
        dx, dy, dc = offset
        to_x = lax.rem(x + turn * dx + 2 * nx_ring, nx_ring)
        to_y = lax.rem(y + turn * dy + 2 * gz, gz)
        to_core = lax.rem(core + dc, 2)
        to = ((to_y // 2) * nx_ring + to_x, lax.rem(to_y, 2) * 2 + to_core)
        return to[0] * gz + to[1], (ix,) + to

    def line(k):
        other = lax.rem(ix + turn * k + 2 * gx, gx)
        return other, (other, iy, iz)

    def row(offset):
        dx, dy = offset
        other = lax.rem(y_high + dy, 2) * nx_ring + lax.rem(x + turn * dx + 2 * nx_ring, nx_ring)
        return other, (ix, other, iz)

    return (ix, iy, iz), plane, line, row


def greet(plane, line):
    barrier = pltpu.get_barrier_semaphore()
    for offset in PLANE_ORDER:
        pl.semaphore_signal(barrier, inc=1, device_id=plane(offset)[1], device_id_type=MESH)
    for offset in LINE_ORDER:
        pl.semaphore_signal(barrier, inc=1, device_id=line(offset)[1], device_id_type=MESH)


def met():
    pl.semaphore_wait(pltpu.get_barrier_semaphore(), len(PLANE_ORDER) + len(LINE_ORDER))


def remote(src, dst, send_sem, recv_sem, device):
    pltpu.make_async_remote_copy(
        src_ref=src,
        dst_ref=dst,
        send_sem=send_sem,
        recv_sem=recv_sem,
        device_id=device,
        device_id_type=MESH,
    ).start()


def settle(ref, sem):
    pltpu.make_async_copy(ref, ref, sem).wait()


def kernel(
    dims,
    beta,
    inc,
    ren,
    w1_hbm,
    w2_hbm,
    w3_hbm,
    rho0,
    heat0,
    sensors,
    thr_out,
    rho_out,
    heat_out,
    code_out,
    most_out,
    inc_v,
    ren_v,
    b_high,
    b_low,
    w1,
    w2,
    w3,
    send1,
    got1,
    send2,
    got2,
    send3,
    got3,
    thr,
    inverse,
    state,
    heat_last,
    rho_last,
    hy_send,
    hy_got,
    hz_send,
    hz_got,
    load_sem,
    out_sem,
    s1_sem,
    r1_sem,
    s2_sem,
    r2_sem,
    s3_sem,
    r3_sem,
    hxs_sem,
    hxr_sem,
    hs_sem,
    hr_sem,
):
    gx, gy, gz, nx, ny, nz = dims
    nd = gy * gz
    sub = nz // nd
    part = sub // CHUNKS
    bx, by, bz = nx // gx, ny // gy, nz // gz
    half = bx // 2
    kx_own = nx // nd
    (ix, iy, iz), plane_device, line_device, row_device = places(gx, gy, gz)
    me = iy * gz + iz
    middle = pl.ds(8, by)

    loads = [
        pltpu.make_async_copy(inc, inc_v, load_sem.at[0]),
        pltpu.make_async_copy(ren, ren_v, load_sem.at[1]),
        pltpu.make_async_copy(w1_hbm, w1, load_sem.at[2]),
        pltpu.make_async_copy(heat0, state.at[0, 0, pl.ds(1, bx), middle, :], load_sem.at[3]),
        pltpu.make_async_copy(rho0, state.at[0, 1, pl.ds(1, bx), middle, :], load_sem.at[4]),
        pltpu.make_async_copy(w2_hbm, w2, load_sem.at[5]),
        pltpu.make_async_copy(w3_hbm, w3, load_sem.at[6]),
    ]
    for load in loads:
        load.start()
    greet(plane_device, line_device)

    lane = lax.broadcasted_iota(jnp.int32, (1, 128), 1)
    sign = jnp.where(lane < 64, -1.0, 1.0).astype(F32)
    first_half = lane < 64

    loads[0].wait()
    loads[1].wait()
    weight = jnp.full((1, 128), beta[0], F32)
    keep = jnp.sqrt(1.0 - weight * weight)[:, :1]
    fresh = weight[:, :1]

    def mix(k, carry):
        for part_of in range(2):
            mixed = keep * inc_v[part_of, k] + fresh * ren_v[part_of, k]
            high, low = split(mixed)
            rows = pl.ds(pl.multiple_of(k * 128 + part_of * 64, 64), 64)
            b_high[rows, :] = high
            b_low[rows, :] = low
        return carry

    lax.fori_loop(0, kx_own, mix, 0)
    loads[2].wait()

    rows1 = nd * part

    def stage1(c):
        flat = send1.at[c].reshape(rows1 * kx_own, 128)
        for q in range(kx_own // 2):
            right = pl.ds(q * 256, 256)
            top = lax.dot_general(w1[c], b_high[right, :], NT, preferred_element_type=F32)
            low = lax.dot_general(
                w1[c, pl.ds(0, 2 * rows1), :], b_low[right, :], NT, preferred_element_type=F32
            )
            total = top[: 2 * rows1] + top[2 * rows1 :] + low
            for side in range(2):
                cut = slice(side * 128, side * 128 + 128)
                cosines = total[:rows1, cut]
                sines = total[rows1:, cut]
                flat[pl.ds(2 * q + side, rows1, stride=kx_own), :] = cosines + sign * pltpu.roll(
                    sines, 64, 1
                )

    def ship1(c):
        for offset in PLANE_ORDER:
            other, device = plane_device(offset)
            remote(
                send1.at[c, pl.ds(other * part, part)],
                got1.at[c, me],
                s1_sem.at[c],
                r1_sem.at[c],
                device,
            )
        pltpu.make_async_copy(
            send1.at[c, pl.ds(me * part, part)], got1.at[c, me], r1_sem.at[c]
        ).start()

    def stage2(c):
        settle(got1.at[c], r1_sem.at[c])
        for p in range(part // 2):
            values = jnp.concatenate(
                [got1[c, :, 2 * p + side].reshape(nx, 128) for side in range(2)], axis=1
            )
            high, low = split(values)
            top = jnp.dot(w2[...], high, preferred_element_type=F32)
            bottom = jnp.dot(w2[pl.ds(0, 2 * nx), :], low, preferred_element_type=F32)
            total = top[: 2 * nx] + top[2 * nx :] + bottom
            for side in range(2):
                cut = slice(side * 128, side * 128 + 128)
                result = total[:nx, cut] + sign * pltpu.roll(total[nx:, cut], 64, 1)
                send2[c, :, 2 * p + side] = result.reshape(gx, bx, 128)
        for k in LINE_ORDER:
            other, device = line_device(k)
            remote(send2.at[c, other], got2.at[c, ix], s2_sem.at[c], r2_sem.at[c], device)
        pltpu.make_async_copy(send2.at[c, ix], got2.at[c, ix], r2_sem.at[c]).start()

    def stage3(c):
        settle(got2.at[c], r2_sem.at[c])
        rows = part * bx
        values = jnp.concatenate([got2[c, g].reshape(rows, 128) for g in range(gx)], axis=1)
        high, low = split(values)
        both = jnp.concatenate([high, low], axis=0)
        for t in range(ny // 256):
            columns = pl.ds(t * 256, 256)
            top = jnp.dot(both, w3[0, :, columns], preferred_element_type=F32)
            field = (
                top[:rows]
                + top[rows:]
                + jnp.dot(high, w3[1, :, columns], preferred_element_type=F32)
            )
            energy = 2.0 + 0.6 * jnp.tanh(field)
            for side in range(2):
                tile = energy[:, side * 128 : side * 128 + 128].reshape(part, 2, half, 128)
                near = tile[:, 0].reshape(part * half, 128)
                far = tile[:, 1].reshape(part * half, 128)
                j = 4 * t + 2 * side
                send3[c, j] = jnp.where(first_half, near, pltpu.roll(far, 64, 1))
                send3[c, j + 1] = jnp.where(first_half, pltpu.roll(near, 64, 1), far)
        target = got3.at[
            pl.ds(pl.multiple_of((iy * sub + c * part) * half, part * half), part * half), :
        ]
        for offset in ROW_ORDER:
            other, device = row_device(offset)
            remote(send3.at[c, other], target, s3_sem.at[0], r3_sem.at[0], device)
        pltpu.make_async_copy(send3.at[c, iy], target, r3_sem.at[0]).start()

    def spot(g, slot):
        return lax.rem(g * SLOTS + slot + bx - 1, bx)

    near_ones = []
    for number, (place, count) in enumerate([(ix, gx), (iy, gy), (iz, gz)]):
        for end in range(2):
            device = [ix, iy, iz]
            device[number] = place + (-1 if end == 0 else 1)
            inner = place > 0 if end == 0 else place < count - 1
            near_ones.append((number, end, inner, tuple(device)))

    outside = jnp.where(lax.rem(lane, 4) < 2, 1.25, 0.0).astype(F32)
    for number, end, inner, device in near_ones:

        @pl.when(jnp.logical_not(inner))
        def _(number=number, end=end):
            for level in range(STEPS):
                if number == 0:
                    x = 0 if end == 0 else bx + 1
                    state[level, 0, x, middle, :] = jnp.full((by, bz), 1.25, F32)
                    state[level, 1, x, middle, :] = jnp.zeros((by, bz), F32)
                elif number == 1:
                    shape = (GROUPS, 1, SLOTS, bz)
                    hy_got[level, end, :, pl.ds(0, 1)] = jnp.full(shape, 1.25, F32)
                    hy_got[level, end, :, pl.ds(1, 1)] = jnp.zeros(shape, F32)
                else:
                    hz_got[level, end] = jnp.broadcast_to(outside, (GROUPS, by, 128))

    def offer(level, g):
        packed = jnp.zeros((by, 128), F32)
        for slot in range(SLOTS):
            x = spot(g, slot) + 1
            heat = state[level, 0, x, middle, :]
            rho = state[level, 1, x, middle, :]
            for f, values in ((0, heat), (1, rho)):
                hy_send[level, 0, g, f, pl.ds(slot, 1), :] = values[:1]
                hy_send[level, 1, g, f, pl.ds(slot, 1), :] = values[by - 1 :]
            ends = jnp.where(lane < 2, pltpu.roll(heat, 1, 1), pltpu.roll(rho, 3, 1))
            if slot:
                ends = pltpu.roll(ends, 4 * slot, 1)
            packed = jnp.where(lane // 4 == slot, ends, packed)
        hz_send[level, g] = packed
        for number, end, inner, device in near_ones:
            if number == 0:
                continue

            @pl.when(inner)
            def _(number=number, end=end, device=device):
                src = hy_send.at[level, end, g] if number == 1 else hz_send.at[level, g]
                dst = (hy_got if number == 1 else hz_got).at[level, 1 - end, g]
                remote(
                    src,
                    dst,
                    hs_sem.at[level, number - 1, end, g],
                    hr_sem.at[level, number - 1, 1 - end, g],
                    device,
                )

    def offer_ends(level):
        for number, end, inner, device in near_ones[:2]:

            @pl.when(inner)
            def _(end=end, device=device):
                remote(
                    state.at[level, :, 1 if end == 0 else bx, middle, :],
                    state.at[level, :, bx + 1 if end == 0 else 0, middle, :],
                    hxs_sem.at[level, end],
                    hxr_sem.at[level, 1 - end],
                    device,
                )

    def accept_ends(level):
        for number, end, inner, device in near_ones[:2]:

            @pl.when(inner)
            def _(end=end):
                settle(
                    state.at[level, :, 0 if end == 0 else bx + 1, middle, :],
                    hxr_sem.at[level, end],
                )

    def accept(level, g):
        for number, end, inner, device in near_ones[2:]:

            @pl.when(inner)
            def _(number=number, end=end):
                settle(
                    (hy_got if number == 1 else hz_got).at[level, end, g],
                    hr_sem.at[level, number - 1, end, g],
                )

        for slot in range(SLOTS):
            x = spot(g, slot) + 1
            for f in range(2):
                row = pl.ds(slot, 1)
                state[level, f, x, pl.ds(7, 1), :] = hy_got[level, 0, g, f, row, :]
                state[level, f, x, pl.ds(8 + by, 1), :] = hy_got[level, 1, g, f, row, :]

    def flux_of(level, g, slot):
        x = spot(g, slot) + 1

        def at(f, dx, dy):
            return state[level, f, x + dx, pl.ds(8 + dy, by), :]

        heat, rho = at(0, 0, 0), at(1, 0, 0)
        cond = rho * rho
        around = [(at(0, dx, dy), at(1, dx, dy)) for dx, dy in ((1, 0), (-1, 0), (0, 1), (0, -1))]
        for end in range(2):
            packed = hz_got[level, end, g]
            edge = 0 if end == 0 else 127
            turn = 1 if end == 0 else 127
            pair = []
            for f, values in ((0, heat), (1, rho)):
                shift = (edge - (4 * slot + 2 * f + end)) % 128
                beyond = pltpu.roll(packed, shift, 1) if shift else packed
                pair.append(jnp.where(lane == edge, beyond, pltpu.roll(values, turn, 1)))
            around.append(tuple(pair))
        flux = None
        for heat_side, rho_side in around:
            term = (cond + rho_side * rho_side) * (heat_side - heat)
            flux = term if flux is None else flux + term
        return x, heat, rho, flux

    def prepare(g, carry):
        accept(0, g)
        for slot in range(SLOTS):
            x, heat, rho, flux = flux_of(0, g, slot)
            state[1, 0, x, middle, :] = heat + 0.08 * flux
            inverse[x - 1] = -1.0 / heat
        return carry

    def first_step(g, carry):
        for slot in range(SLOTS):
            x = spot(g, slot)
            rho = state[0, 1, x + 1, middle, :]
            growth = jnp.exp(thr[x] * inverse[x]) * (1.0 - rho)
            state[1, 0, x + 1, middle, :] = state[1, 0, x + 1, middle, :] + 0.48 * growth
            state[1, 1, x + 1, middle, :] = rho + 0.64 * growth
        offer(1, g)

        @pl.when(g == 0)
        def _():
            offer_ends(1)

        return carry

    def later_step(level):
        def group(g, carry):
            @pl.when(g == 0)
            def _():
                accept_ends(level)

            accept(level, g)
            for slot in range(SLOTS):
                x, heat, rho, flux = flux_of(level, g, slot)
                growth = jnp.exp(-thr[x - 1] / heat) * (1.0 - rho)
                new_heat = heat + 0.16 * (0.5 * flux + 3.0 * growth)
                new_rho = rho + 0.64 * growth
                if level + 1 < STEPS:
                    state[level + 1, 0, x, middle, :] = new_heat
                    state[level + 1, 1, x, middle, :] = new_rho
                else:
                    heat_last[x - 1] = new_heat
                    rho_last[x - 1] = new_rho
            if level + 1 < STEPS:
                offer(level + 1, g)

                @pl.when(g == 0)
                def _():
                    offer_ends(level + 1)

            return carry

        lax.fori_loop(0, GROUPS, group, 0)

    def offer_first(g, carry):
        offer(0, g)
        return carry

    def locate():
        x = sensors[0:1, :] - ix * bx
        y = sensors[1:2, :] - iy * by
        z = sensors[2:3, :] - iz * bz
        own = (x >= 0) & (x < bx) & (y >= 0) & (y < by) & (z >= 0) & (z < bz)
        code = jnp.where(own, (x * by + y) * bz + z, -1)
        code_out[...] = code
        width = most_out.shape[1]
        most = code[:, :width]
        for k in range(1, S // width):
            most = jnp.maximum(most, code[:, k * width : (k + 1) * width])
        most_out[...] = most

    stage1(0)
    met()

    def pipeline(i, carry):
        @pl.when((i > 0) & (i < CHUNKS))
        def _():
            stage1(i)

        @pl.when(i < CHUNKS)
        def _():
            ship1(i)

        @pl.when(i == 0)
        def _():
            loads[3].wait()
            loads[4].wait()
            offer_ends(0)
            lax.fori_loop(0, GROUPS, offer_first, 0)
            loads[5].wait()
            loads[6].wait()

        @pl.when((i >= 1) & (i <= CHUNKS))
        def _():
            stage2(i - 1)

        @pl.when(i == 2)
        def _():
            locate()
            accept_ends(0)

        @pl.when((i >= 2) & (i < 2 + GROUPS))
        def _():
            prepare(i - 2, 0)

        @pl.when(i >= LAG)
        def _():
            stage3(i - LAG)

        return carry

    lax.fori_loop(0, CHUNKS + LAG, pipeline, 0)

    settle(got3, r3_sem.at[0])
    for x in range(half):
        turned = got3[pl.ds(x, bz, stride=half), :].T
        thr[x] = turned[:by]
        thr[half + x] = turned[by:]
    thr_copy = pltpu.make_async_copy(thr, thr_out, out_sem.at[0])
    thr_copy.start()

    lax.fori_loop(0, GROUPS, first_step, 0)
    for level in range(1, STEPS):
        later_step(level)
    heat_copy = pltpu.make_async_copy(heat_last, heat_out, out_sem.at[1])
    rho_copy = pltpu.make_async_copy(rho_last, rho_out, out_sem.at[2])
    heat_copy.start()
    rho_copy.start()

    def drain_chunk(c, carry):
        settle(send1.at[c, pl.ds(0, (nd - 1) * part)], s1_sem.at[c])
        settle(send2.at[c, pl.ds(0, gx - 1)], s2_sem.at[c])
        return carry

    lax.fori_loop(0, CHUNKS, drain_chunk, 0)
    settle(send3.at[:, pl.ds(0, gy - 1)], s3_sem.at[0])
    for number, end, inner, device in near_ones:

        @pl.when(inner)
        def _(number=number, end=end):
            for level in range(STEPS):
                if number == 0:
                    settle(
                        state.at[level, :, 1 if end == 0 else bx, middle, :],
                        hxs_sem.at[level, end],
                    )
                    continue
                for g in range(GROUPS):
                    settle(
                        hy_send.at[level, end, g] if number == 1 else hz_send.at[level, g],
                        hs_sem.at[level, number - 1, end, g],
                    )

    thr_copy.wait()
    heat_copy.wait()
    rho_copy.wait()


def read_kernel(
    by, code, most, thr, rho, heat, thr_out, rho_out, heat_out, found, thr_v, rho_v, heat_v, sem
):
    ins = [
        pltpu.make_async_copy(src, dst, sem.at[k])
        for k, (src, dst) in enumerate(((heat, heat_v), (thr, thr_v), (rho, rho_v)))
    ]
    outs = [
        pltpu.make_async_copy(src, dst, sem.at[3 + k])
        for k, (src, dst) in enumerate(((heat_v, heat_out), (thr_v, thr_out), (rho_v, rho_out)))
    ]
    for copy in ins:
        copy.start()
    found[...] = jnp.zeros(found.shape, F32)
    for copy, after in zip(ins, outs):
        copy.wait()
        after.start()
    lane = lax.broadcasted_iota(jnp.int32, (1, 128), 1)
    width = most.shape[1]

    def column(j, carry):
        @pl.when(most[0, j] >= 0)
        def _():
            def one(k, carry):
                s = k * width + j
                cell = code[0, s]

                @pl.when(cell >= 0)
                def _():
                    row = heat_v[cell // (128 * by), pl.ds(lax.rem(cell // 128, by), 1), :]
                    where = lax.rem(s, 128)
                    turned = pltpu.roll(row, lax.rem(where - lax.rem(cell, 128) + 128, 128), 1)
                    target = pl.ds(s // 512 * 8 + lax.rem(s // 128, 4), 1)
                    found[target, :] = jnp.where(lane == where, turned, found[target, :])

                return carry

            lax.fori_loop(0, S // width, one, 0)

        return carry

    lax.fori_loop(0, width, column, 0)
    for copy in outs:
        copy.wait()


def sum_kernel(
    dims, cost, found, recorded, model_out, odds_out, send, red_a, red_mid, red_b, red_fin, red_c,
    rs_sem, rr_sem,
):
    gx, gy, gz = dims
    (ix, iy, iz), plane_device, line_device, _ = places(gx, gy, gz)
    me = iy * gz + iz
    per = S // 128 // gx
    greet(plane_device, line_device)
    for block in range(gx):
        send[block] = found[pl.ds(block * 8, 8), :]
    met()
    for k in LINE_ORDER:
        other, device = line_device(k)
        remote(send.at[other], red_a.at[ix], rs_sem.at[0], rr_sem.at[0], device)
    pltpu.make_async_copy(send.at[ix], red_a.at[ix], rr_sem.at[0]).start()
    settle(red_a, rr_sem.at[0])
    red_mid[...] = jnp.sum(red_a[...], axis=0)
    for offset in PLANE_ORDER:
        remote(red_mid, red_b.at[me], rs_sem.at[1], rr_sem.at[1], plane_device(offset)[1])
    pltpu.make_async_copy(red_mid, red_b.at[me], rr_sem.at[1]).start()
    settle(red_b, rr_sem.at[1])
    red_fin[...] = jnp.sum(red_b[...], axis=0)
    for k in LINE_ORDER:
        remote(red_fin, red_c.at[ix], rs_sem.at[2], rr_sem.at[2], line_device(k)[1])
    pltpu.make_async_copy(red_fin, red_c.at[ix], rr_sem.at[2]).start()
    settle(red_c, rr_sem.at[2])
    misfit = jnp.zeros((per, 128), F32)
    for block in range(gx):
        values = red_c[block, pl.ds(0, per), :]
        model_out[pl.ds(block * per, per), :] = values
        gap = (values - recorded[pl.ds(block * per, per), :]) / 0.2
        misfit = misfit + gap * gap
    odds_out[0] = cost[0] - 0.5 * (jnp.sum(misfit) / S)
    settle(red_a.at[pl.ds(0, gx - 1)], rs_sem.at[0])
    settle(red_b.at[pl.ds(0, gy * gz - 1)], rs_sem.at[1])
    settle(red_c.at[pl.ds(0, gx - 1)], rs_sem.at[2])


def solution(mesh):
    gx, gy, gz = (mesh.shape[name] for name in ("gx", "gy", "gz"))
    nx, ny, nz = MESH_EXTENT_EAST, MESH_EXTENT_NORTH, MESH_EXTENT_UPWARD
    depth, first, second = tables(gx, gy, gz, nx, ny, nz)
    nd = gy * gz
    sub = nz // nd
    part = sub // CHUNKS
    bx, by, bz = nx // gx, ny // gy, nz // gz
    kx_own, ky_own = nx // nd, ny // gx
    smem = pl.BlockSpec(memory_space=pltpu.SMEM)
    hbm = pl.BlockSpec(memory_space=pl.ANY)
    vmem = pl.BlockSpec(memory_space=pltpu.VMEM)
    dma = pltpu.SemaphoreType.DMA
    block = jax.ShapeDtypeStruct((bx, by, bz), F32)

    def body(incumbent, renewed, beta, rho, heat, place, recorded, cost):
        energy, density, kelvin, code, most = pl.pallas_call(
            functools.partial(kernel, (gx, gy, gz, nx, ny, nz)),
            out_shape=(
                block,
                block,
                block,
                jax.ShapeDtypeStruct((1, S), jnp.int32),
                jax.ShapeDtypeStruct((1, 256), jnp.int32),
            ),
            in_specs=[smem] + [hbm] * 7 + [vmem],
            out_specs=(hbm, hbm, hbm, vmem, vmem),
            scratch_shapes=[
                pltpu.VMEM((2, kx_own, ky_own, nz), F32),
                pltpu.VMEM((2, kx_own, ky_own, nz), F32),
                pltpu.VMEM((kx_own * 2 * ky_own, nz), BF16),
                pltpu.VMEM((kx_own * 2 * ky_own, nz), BF16),
                pltpu.VMEM(depth.shape, BF16),
                pltpu.VMEM(first.shape, BF16),
                pltpu.VMEM(second.shape, BF16),
                pltpu.VMEM((CHUNKS, nd * part, kx_own, 128), F32),
                pltpu.VMEM((CHUNKS, nd, part, kx_own, 128), F32),
                pltpu.VMEM((CHUNKS, gx, part, bx, 128), F32),
                pltpu.VMEM((CHUNKS, gx, part, bx, 128), F32),
                pltpu.VMEM((CHUNKS, gy, part * bx // 2, 128), F32),
                pltpu.VMEM((bz * bx // 2, 128), F32),
                pltpu.VMEM((bx, by, bz), F32),
                pltpu.VMEM((bx, by, bz), F32),
                pltpu.VMEM((STEPS, 2, bx + 2, by + 16, bz), F32),
                pltpu.VMEM((bx, by, bz), F32),
                pltpu.VMEM((bx, by, bz), F32),
                pltpu.VMEM((STEPS, 2, GROUPS, 2, SLOTS, bz), F32),
                pltpu.VMEM((STEPS, 2, GROUPS, 2, SLOTS, bz), F32),
                pltpu.VMEM((STEPS, GROUPS, by, bz), F32),
                pltpu.VMEM((STEPS, 2, GROUPS, by, bz), F32),
                dma((7,)),
                dma((3,)),
                dma((CHUNKS,)),
                dma((CHUNKS,)),
                dma((CHUNKS,)),
                dma((CHUNKS,)),
                dma((1,)),
                dma((1,)),
                dma((STEPS, 2)),
                dma((STEPS, 2)),
                dma((STEPS, 2, 2, GROUPS)),
                dma((STEPS, 2, 2, GROUPS)),
            ],
            compiler_params=pltpu.CompilerParams(
                collective_id=0, has_side_effects=True, vmem_limit_bytes=56 * 1024 * 1024
            ),
            cost_estimate=pl.CostEstimate(
                flops=7_000_000_000, bytes_accessed=16_000_000, transcendentals=1_000_000
            ),
        )(
            beta,
            incumbent,
            renewed,
            jnp.asarray(depth),
            jnp.asarray(first),
            jnp.asarray(second),
            rho,
            heat,
            place.T,
        )
        energy, density, kelvin, found = pl.pallas_call(
            functools.partial(read_kernel, by),
            out_shape=(block, block, block, jax.ShapeDtypeStruct((gx * 8, 128), F32)),
            in_specs=[smem] * 2 + [hbm] * 3,
            out_specs=(hbm, hbm, hbm, vmem),
            scratch_shapes=[pltpu.VMEM((bx, by, bz), F32)] * 3 + [dma((6,))],
            compiler_params=pltpu.CompilerParams(vmem_limit_bytes=16 * 1024 * 1024),
        )(code, most, energy, density, kelvin)
        model, odds = pl.pallas_call(
            functools.partial(sum_kernel, (gx, gy, gz)),
            out_shape=(
                jax.ShapeDtypeStruct((S // 128, 128), F32),
                jax.ShapeDtypeStruct((1,), F32),
            ),
            in_specs=[smem, vmem, vmem],
            out_specs=(vmem, smem),
            scratch_shapes=[
                pltpu.VMEM((gx, 8, 128), F32),
                pltpu.VMEM((gx, 8, 128), F32),
                pltpu.VMEM((8, 128), F32),
                pltpu.VMEM((nd, 8, 128), F32),
                pltpu.VMEM((8, 128), F32),
                pltpu.VMEM((gx, 8, 128), F32),
                dma((3,)),
                dma((3,)),
            ],
            compiler_params=pltpu.CompilerParams(collective_id=1, has_side_effects=True),
        )(cost, found, recorded.reshape(S // 128, 128))
        return energy, density, kelvin, model.reshape(S), odds

    return jax.shard_map(
        body,
        mesh=mesh,
        in_specs=(
            P(None, ("gy", "gz"), "gx", None),
            P(None, ("gy", "gz"), "gx", None),
            P(),
            P("gx", "gy", "gz"),
            P("gx", "gy", "gz"),
            P(),
            P(),
            P(),
        ),
        out_specs=(P("gx", "gy", "gz"), P("gx", "gy", "gz"), P("gx", "gy", "gz"), P(), P()),
        check_vma=False,
    )
```

time: 158 us -> 129 us (0.82)
  Pallas kernels: 146 us -> 118 us
  other arithmetic: 3.27 us -> 0 us
  local copies, waits for them, and re-layouts: 5.01 us -> 6.96 us
    pallas_call x1, Pallas kernels: 146 us -> 86.8 us  [body(): pl.pallas_call(functools.partial(kernel, (gx, gy, gz, nx, ny, nz)), out_s...]
    pallas_call x0 -> x2, Pallas kernels: none -> 31.2 us  [the longest x1 22.1 us: body(): pl.pallas_call(functools.partial(sum_kernel, (gx, gy, gz)), out_shape=(ja...]
    unnamed x10 -> x13, local copies, waits for them, and re-layouts: 5.01 us -> 6.96 us
    sub x1 -> x0, other arithmetic: 1.65 us -> none  [body(): local_z = place[:, 2] - lax.axis_index('gz') * bz]
where the time goes in v2:
time: 129 us
  Pallas kernels  118 us (91%)
  local copies, waits for them, and re-layouts  6.96 us (5%)
  between operations  3.73 us (3%)
    pallas_call x1, Pallas kernels, body(): pl.pallas_call(functools.partial(kernel, (gx, gy, gz, nx, ny, nz)), out_s...  86.8 us
    pallas_call x1, Pallas kernels, body(): pl.pallas_call(functools.partial(sum_kernel, (gx, gy, gz)), out_shape=(ja...  22.1 us
    pallas_call x1, Pallas kernels, body(): pl.pallas_call(functools.partial(read_kernel, by), out_shape=(block, bloc...  9.11 us
    unnamed x13, local copies, waits for them, and re-layouts  6.96 us

profile of v2, /device:TPU:1, one launch (start us, length us, event | category | flops | bytes accessed | tf_op | source)
XLA Modules:
  0.0 128.6 jit_solution(17968992057081996467)
XLA Ops:
  1.3 86.8 %shard_map.146 = (f32[32,64,128]{2,1,0:T(8,128)}, f32[32,64,128]{2,1,0:T(8,128)}, f32[32,64,128]{2,1,0:T(8,128)}, s32[1,4096]{1,0:T(1,128)}, s32[1,256]{1,0:T(1,128)}) custom-call(f32[1]{0:T(128)S(6)} %copy.18.beta, f32[2,8,64,512]{3,2,1,0:T(8,128)} %inc.1, f32[2,8,64,512]{3,2,1,0:T(8,128)} %ren.1, bf16[8,256,512]{2,1,0:T(8,128)(2,1)} %constant.6.clone.w1_hbm, ...), custom_call_target="tpu_custom_call" | custom-call | flops 7000000000 | bytes 16000000 | tf_op jit(solution)/shard_map/pallas_call | solution.py:705
  88.0 0.0 copy-start
  88.1 1.2 copy-done
  89.3 0.0 copy-start.1
  89.3 1.2 copy-done.1
  90.5 0.0 copy-start.2
  90.5 1.2 copy-done.2
  91.7 0.0 copy-start.4
  91.7 0.7 copy-done.4
  92.4 0.0 copy-start.5
  92.4 0.7 copy-done.5
  93.1 9.1 %shard_map.147 = (f32[32,64,128]{2,1,0:T(8,128)}, f32[32,64,128]{2,1,0:T(8,128)}, f32[32,64,128]{2,1,0:T(8,128)}, f32[64,128]{1,0:T(8,128)S(1)}) custom-call(s32[1,4096]{1,0:T(1,128)S(1)} %copy-done.4, s32[1,256]{1,0:T(1,128)S(1)} %copy-done.5, f32[32,64,128]{2,1,0:T(8,128)S(1)} %copy-done, f32[32,64,128]{2,1,0:T(8,128)S(1)} %copy-done.1, ...), custom_call_target="tpu_custom_call" | custom-call | tf_op jit(solution)/shard_map/pallas_call | solution.py:769
  102.2 0.0 copy-start.3
  102.2 0.6 copy-done.3
  103.5 22.1 %shard_map.148 = (f32[32,128]{1,0:T(8,128)}, f32[1]{0:T(128)}) custom-call(f32[1]{0:T(128)S(6)} %copy.19.cost, f32[64,128]{1,0:T(8,128)} %copy-done.3, f32[32,128]{1,0:T(8,128)} %bitcast.3), custom_call_target="tpu_custom_call" | custom-call | tf_op jit(solution)/shard_map/pallas_call | solution.py:777
  125.5 1.3 %copy.20 = f32[4096]{0:T(1024)} copy(f32[4096]{0:T(1024)} %bitcast.4) | data formatting | bytes 32768
Async XLA Ops:
  88.0 1.2 copy-start
  89.3 1.2 copy-start.1
  90.5 1.2 copy-start.2
  91.7 0.7 copy-start.4
  92.4 0.7 copy-start.5
  102.2 0.6 copy-start.3

commit v3 on v2

--- a/solution.py
+++ b/solution.py
@@ -19,6 +19,7 @@
 LAG = 3
 GROUPS = 4
 SLOTS = 8
+PIECE = 32
 ABL = set()
 MESH = pl.DeviceIdType.MESH
 F32 = jnp.float32
@@ -158,7 +159,6 @@
     rho_out,
     heat_out,
     code_out,
-    most_out,
     inc_v,
     ren_v,
     b_high,
@@ -176,7 +176,7 @@
     inverse,
     state,
     heat_last,
-    rho_last,
+    rho_v,
     hy_send,
     hy_got,
     hz_send,
@@ -210,7 +210,7 @@
         pltpu.make_async_copy(ren, ren_v, load_sem.at[1]),
         pltpu.make_async_copy(w1_hbm, w1, load_sem.at[2]),
         pltpu.make_async_copy(heat0, state.at[0, 0, pl.ds(1, bx), middle, :], load_sem.at[3]),
-        pltpu.make_async_copy(rho0, state.at[0, 1, pl.ds(1, bx), middle, :], load_sem.at[4]),
+        pltpu.make_async_copy(rho0, rho_v, load_sem.at[4]),
         pltpu.make_async_copy(w2_hbm, w2, load_sem.at[5]),
         pltpu.make_async_copy(w3_hbm, w3, load_sem.at[6]),
     ]
@@ -355,11 +355,11 @@
         for slot in range(SLOTS):
             x = spot(g, slot) + 1
             heat = state[level, 0, x, middle, :]
-            rho = state[level, 1, x, middle, :]
-            for f, values in ((0, heat), (1, rho)):
+            cond = state[level, 1, x, middle, :]
+            for f, values in ((0, heat), (1, cond)):
                 hy_send[level, 0, g, f, pl.ds(slot, 1), :] = values[:1]
                 hy_send[level, 1, g, f, pl.ds(slot, 1), :] = values[by - 1 :]
-            ends = jnp.where(lane < 2, pltpu.roll(heat, 1, 1), pltpu.roll(rho, 3, 1))
+            ends = jnp.where(lane < 2, pltpu.roll(heat, 1, 1), pltpu.roll(cond, 3, 1))
             if slot:
                 ends = pltpu.roll(ends, 4 * slot, 1)
             packed = jnp.where(lane // 4 == slot, ends, packed)
@@ -420,46 +420,50 @@
                 state[level, f, x, pl.ds(7, 1), :] = hy_got[level, 0, g, f, row, :]
                 state[level, f, x, pl.ds(8 + by, 1), :] = hy_got[level, 1, g, f, row, :]
 
-    def flux_of(level, g, slot):
+    pieces = [pl.ds(k * PIECE, PIECE) for k in range(by // PIECE)]
+
+    def flux_of(level, g, slot, piece):
         x = spot(g, slot) + 1
 
         def at(f, dx, dy):
-            return state[level, f, x + dx, pl.ds(8 + dy, by), :]
-
-        heat, rho = at(0, 0, 0), at(1, 0, 0)
-        cond = rho * rho
+            return state[level, f, x + dx, pl.ds(8 + piece.start + dy, PIECE), :]
+
+        heat, cond = at(0, 0, 0), at(1, 0, 0)
         around = [(at(0, dx, dy), at(1, dx, dy)) for dx, dy in ((1, 0), (-1, 0), (0, 1), (0, -1))]
         for end in range(2):
-            packed = hz_got[level, end, g]
+            packed = hz_got[level, end, g, piece, :]
             edge = 0 if end == 0 else 127
             turn = 1 if end == 0 else 127
             pair = []
-            for f, values in ((0, heat), (1, rho)):
+            for f, values in ((0, heat), (1, cond)):
                 shift = (edge - (4 * slot + 2 * f + end)) % 128
                 beyond = pltpu.roll(packed, shift, 1) if shift else packed
                 pair.append(jnp.where(lane == edge, beyond, pltpu.roll(values, turn, 1)))
             around.append(tuple(pair))
         flux = None
-        for heat_side, rho_side in around:
-            term = (cond + rho_side * rho_side) * (heat_side - heat)
+        for heat_side, cond_side in around:
+            term = (cond + cond_side) * (heat_side - heat)
             flux = term if flux is None else flux + term
-        return x, heat, rho, flux
+        return x, heat, flux
 
     def prepare(g, carry):
         accept(0, g)
         for slot in range(SLOTS):
-            x, heat, rho, flux = flux_of(0, g, slot)
-            state[1, 0, x, middle, :] = heat + 0.08 * flux
-            inverse[x - 1] = -1.0 / heat
+            for piece in pieces:
+                x, heat, flux = flux_of(0, g, slot, piece)
+                state[1, 0, x, pl.ds(8 + piece.start, PIECE), :] = heat + 0.08 * flux
+                inverse[x - 1, piece, :] = -1.0 / heat
         return carry
 
     def first_step(g, carry):
         for slot in range(SLOTS):
             x = spot(g, slot)
-            rho = state[0, 1, x + 1, middle, :]
+            rho = rho_v[x]
             growth = jnp.exp(thr[x] * inverse[x]) * (1.0 - rho)
             state[1, 0, x + 1, middle, :] = state[1, 0, x + 1, middle, :] + 0.48 * growth
-            state[1, 1, x + 1, middle, :] = rho + 0.64 * growth
+            rho = rho + 0.64 * growth
+            rho_v[x] = rho
+            state[1, 1, x + 1, middle, :] = rho * rho
         offer(1, g)
 
         @pl.when(g == 0)
@@ -476,16 +480,19 @@
 
             accept(level, g)
             for slot in range(SLOTS):
-                x, heat, rho, flux = flux_of(level, g, slot)
-                growth = jnp.exp(-thr[x - 1] / heat) * (1.0 - rho)
-                new_heat = heat + 0.16 * (0.5 * flux + 3.0 * growth)
-                new_rho = rho + 0.64 * growth
-                if level + 1 < STEPS:
-                    state[level + 1, 0, x, middle, :] = new_heat
-                    state[level + 1, 1, x, middle, :] = new_rho
-                else:
-                    heat_last[x - 1] = new_heat
-                    rho_last[x - 1] = new_rho
+                for piece in pieces:
+                    x, heat, flux = flux_of(level, g, slot, piece)
+                    rho = rho_v[x - 1, piece, :]
+                    growth = jnp.exp(-thr[x - 1, piece, :] / heat) * (1.0 - rho)
+                    heat = heat + (0.08 * flux + 0.48 * growth)
+                    rho = rho + 0.64 * growth
+                    rho_v[x - 1, piece, :] = rho
+                    if level + 1 < STEPS:
+                        rows = pl.ds(8 + piece.start, PIECE)
+                        state[level + 1, 0, x, rows, :] = heat
+                        state[level + 1, 1, x, rows, :] = rho * rho
+                    else:
+                        heat_last[x - 1, piece, :] = heat
             if level + 1 < STEPS:
                 offer(level + 1, g)
 
@@ -496,6 +503,11 @@
             return carry
 
         lax.fori_loop(0, GROUPS, group, 0)
+
+    def conduct(x, carry):
+        rho = rho_v[x]
+        state[0, 1, x + 1, middle, :] = rho * rho
+        return carry
 
     def offer_first(g, carry):
         offer(0, g)
@@ -507,12 +519,12 @@
         z = sensors[2:3, :] - iz * bz
         own = (x >= 0) & (x < bx) & (y >= 0) & (y < by) & (z >= 0) & (z < bz)
         code = jnp.where(own, (x * by + y) * bz + z, -1)
-        code_out[...] = code
-        width = most_out.shape[1]
-        most = code[:, :width]
-        for k in range(1, S // width):
-            most = jnp.maximum(most, code[:, k * width : (k + 1) * width])
-        most_out[...] = most
+        cells = [code[:, t * 128 : t * 128 + 128] for t in range(S // 128)]
+        last_one = functools.reduce(
+            jnp.maximum, [jnp.where(c >= 0, c + t * (bx * by * bz), -1) for t, c in enumerate(cells)]
+        )
+        count = functools.reduce(jnp.add, [jnp.where(c >= 0, 1, 0) for c in cells])
+        code_out[...] = jnp.concatenate([code, last_one, count], axis=1)
 
     stage1(0)
     met()
@@ -530,6 +542,7 @@
         def _():
             loads[3].wait()
             loads[4].wait()
+            lax.fori_loop(0, bx, conduct, 0)
             offer_ends(0)
             lax.fori_loop(0, GROUPS, offer_first, 0)
             loads[5].wait()
@@ -568,7 +581,7 @@
     for level in range(1, STEPS):
         later_step(level)
     heat_copy = pltpu.make_async_copy(heat_last, heat_out, out_sem.at[1])
-    rho_copy = pltpu.make_async_copy(rho_last, rho_out, out_sem.at[2])
+    rho_copy = pltpu.make_async_copy(rho_v, rho_out, out_sem.at[2])
     heat_copy.start()
     rho_copy.start()
 
@@ -602,8 +615,9 @@
 
 
 def read_kernel(
-    by, code, most, thr, rho, heat, thr_out, rho_out, heat_out, found, thr_v, rho_v, heat_v, sem
+    by, code_hbm, thr, rho, heat, thr_out, rho_out, heat_out, found, code, thr_v, rho_v, heat_v, sem
 ):
+    codes = pltpu.make_async_copy(code_hbm, code, sem.at[6])
     ins = [
         pltpu.make_async_copy(src, dst, sem.at[k])
         for k, (src, dst) in enumerate(((heat, heat_v), (thr, thr_v), (rho, rho_v)))
@@ -612,78 +626,106 @@
         pltpu.make_async_copy(src, dst, sem.at[3 + k])
         for k, (src, dst) in enumerate(((heat_v, heat_out), (thr_v, thr_out), (rho_v, rho_out)))
     ]
+    codes.start()
     for copy in ins:
         copy.start()
     found[...] = jnp.zeros(found.shape, F32)
+    lane = lax.broadcasted_iota(jnp.int32, (1, 128), 1)
     for copy, after in zip(ins, outs):
         copy.wait()
         after.start()
-    lane = lax.broadcasted_iota(jnp.int32, (1, 128), 1)
-    width = most.shape[1]
-
-    def column(j, carry):
-        @pl.when(most[0, j] >= 0)
+    codes.wait()
+
+    block = heat_v.shape[0] * by * 128
+
+    def read(t, j):
+        cell = jnp.bitwise_and(code[0, t * 128 + j], block - 1)
+        place = jnp.right_shift(cell, 7)
+        row = heat_v[place // by, pl.ds(lax.rem(place, by), 1), :]
+        turned = pltpu.roll(row, jnp.bitwise_and(j - cell, 127), 1)
+        target = pl.ds(t, 1)
+        found[target, :] = jnp.where(lane == j, turned, found[target, :])
+
+    def quad(q, carry):
+        lasts = [code[0, S + 4 * q + t] for t in range(4)]
+
+        @pl.when(functools.reduce(jnp.maximum, lasts) >= 0)
         def _():
-            def one(k, carry):
-                s = k * width + j
-                cell = code[0, s]
-
-                @pl.when(cell >= 0)
+            def column(j, carry):
+                final = code[0, S + j]
+
+                @pl.when(final >= 0)
                 def _():
-                    row = heat_v[cell // (128 * by), pl.ds(lax.rem(cell // 128, by), 1), :]
-                    where = lax.rem(s, 128)
-                    turned = pltpu.roll(row, lax.rem(where - lax.rem(cell, 128) + 128, 128), 1)
-                    target = pl.ds(s // 512 * 8 + lax.rem(s // 128, 4), 1)
-                    found[target, :] = jnp.where(lane == where, turned, found[target, :])
+                    number = jnp.right_shift(final, block.bit_length() - 1)
+                    alone = code[0, S + 128 + j] == 1
+
+                    def one(t, carry):
+                        @pl.when(code[0, t * 128 + j] >= 0)
+                        def _():
+                            read(t, j)
+
+                        return carry
+
+                    lax.fori_loop(jnp.where(alone, number, 0), number + 1, one, 0)
 
                 return carry
 
-            lax.fori_loop(0, S // width, one, 0)
+            lax.fori_loop(4 * q, 4 * q + 4, column, 0)
 
         return carry
 
-    lax.fori_loop(0, width, column, 0)
+    lax.fori_loop(0, 32, quad, 0)
     for copy in outs:
         copy.wait()
 
 
 def sum_kernel(
-    dims, cost, found, recorded, model_out, odds_out, send, red_a, red_mid, red_b, red_fin, red_c,
-    rs_sem, rr_sem,
+    dims, cost, found, recorded, model_out, odds_out, red_a, mid_b, red_b, mid_c, red_c, mid_d,
+    red_d, rs_sem, rr_sem,
 ):
     gx, gy, gz = dims
-    (ix, iy, iz), plane_device, line_device, _ = places(gx, gy, gz)
-    me = iy * gz + iz
-    per = S // 128 // gx
-    greet(plane_device, line_device)
-    for block in range(gx):
-        send[block] = found[pl.ds(block * 8, 8), :]
-    met()
-    for k in LINE_ORDER:
-        other, device = line_device(k)
-        remote(send.at[other], red_a.at[ix], rs_sem.at[0], rr_sem.at[0], device)
-    pltpu.make_async_copy(send.at[ix], red_a.at[ix], rr_sem.at[0]).start()
-    settle(red_a, rr_sem.at[0])
-    red_mid[...] = jnp.sum(red_a[...], axis=0)
-    for offset in PLANE_ORDER:
-        remote(red_mid, red_b.at[me], rs_sem.at[1], rr_sem.at[1], plane_device(offset)[1])
-    pltpu.make_async_copy(red_mid, red_b.at[me], rr_sem.at[1]).start()
-    settle(red_b, rr_sem.at[1])
-    red_fin[...] = jnp.sum(red_b[...], axis=0)
-    for k in LINE_ORDER:
-        remote(red_fin, red_c.at[ix], rs_sem.at[2], rr_sem.at[2], line_device(k)[1])
-    pltpu.make_async_copy(red_fin, red_c.at[ix], rr_sem.at[2]).start()
-    settle(red_c, rr_sem.at[2])
-    misfit = jnp.zeros((per, 128), F32)
-    for block in range(gx):
-        values = red_c[block, pl.ds(0, per), :]
-        model_out[pl.ds(block * per, per), :] = values
-        gap = (values - recorded[pl.ds(block * per, per), :]) / 0.2
-        misfit = misfit + gap * gap
-    odds_out[0] = cost[0] - 0.5 * (jnp.sum(misfit) / S)
-    settle(red_a.at[pl.ds(0, gx - 1)], rs_sem.at[0])
-    settle(red_b.at[pl.ds(0, gy * gz - 1)], rs_sem.at[1])
-    settle(red_c.at[pl.ds(0, gx - 1)], rs_sem.at[2])
+    (ix, iy, iz), _, line_device, row_device = places(gx, gy, gz)
+    per = S // 128 // gz
+    lines = [line_device(k) for k in LINE_ORDER]
+    rows = [row_device(offset) for offset in ROW_ORDER]
+    quads = [lax.rem(iz + k, gz) for k in (2, 1, 3)]
+    quads = [(other, (ix, iy, other)) for other in quads]
+    barrier = pltpu.get_barrier_semaphore()
+    partners = lines + rows + quads
+    for _, device in partners:
+        pl.semaphore_signal(barrier, inc=1, device_id=device, device_id_type=MESH)
+
+    def piece(k):
+        return pl.ds(pl.multiple_of(k * per, per), per)
+
+    red_a[iz] = found[piece(iz), :]
+    pl.semaphore_wait(barrier, len(partners))
+    for other, device in quads:
+        remote(found.at[piece(other), :], red_a.at[iz], rs_sem.at[0], rr_sem.at[0], device)
+    settle(red_a.at[pl.ds(0, gz - 1)], rr_sem.at[0])
+    mid_b[...] = jnp.sum(red_a[...], axis=0)
+    for other, device in lines:
+        remote(mid_b, red_b.at[ix], rs_sem.at[1], rr_sem.at[1], device)
+    red_b[ix] = mid_b[...]
+    settle(red_b.at[pl.ds(0, gx - 1)], rr_sem.at[1])
+    mid_c[...] = jnp.sum(red_b[...], axis=0)
+    for other, device in rows:
+        remote(mid_c, red_c.at[iy], rs_sem.at[2], rr_sem.at[2], device)
+    red_c[iy] = mid_c[...]
+    settle(red_c.at[pl.ds(0, gy - 1)], rr_sem.at[2])
+    mid_d[...] = jnp.sum(red_c[...], axis=0)
+    for other, device in quads:
+        remote(mid_d, red_d.at[iz], rs_sem.at[3], rr_sem.at[3], device)
+    red_d[iz] = mid_d[...]
+    settle(red_d.at[pl.ds(0, gz - 1)], rr_sem.at[3])
+    values = red_d[...].reshape(S // 128, 128)
+    model_out[...] = values
+    gap = (values - recorded[...]) / 0.2
+    odds_out[0] = cost[0] - 0.5 * (jnp.sum(gap * gap) / S)
+    settle(red_a.at[pl.ds(0, gz - 1)], rs_sem.at[0])
+    settle(red_b.at[pl.ds(0, gx - 1)], rs_sem.at[1])
+    settle(red_c.at[pl.ds(0, gy - 1)], rs_sem.at[2])
+    settle(red_d.at[pl.ds(0, gz - 1)], rs_sem.at[3])
 
 
 def solution(mesh):
@@ -695,6 +737,7 @@
     part = sub // CHUNKS
     bx, by, bz = nx // gx, ny // gy, nz // gz
     kx_own, ky_own = nx // nd, ny // gx
+    per = S // 128 // gz
     smem = pl.BlockSpec(memory_space=pltpu.SMEM)
     hbm = pl.BlockSpec(memory_space=pl.ANY)
     vmem = pl.BlockSpec(memory_space=pltpu.VMEM)
@@ -702,17 +745,16 @@
     block = jax.ShapeDtypeStruct((bx, by, bz), F32)
 
     def body(incumbent, renewed, beta, rho, heat, place, recorded, cost):
-        energy, density, kelvin, code, most = pl.pallas_call(
+        energy, density, kelvin, code = pl.pallas_call(
             functools.partial(kernel, (gx, gy, gz, nx, ny, nz)),
             out_shape=(
                 block,
                 block,
                 block,
-                jax.ShapeDtypeStruct((1, S), jnp.int32),
-                jax.ShapeDtypeStruct((1, 256), jnp.int32),
+                jax.ShapeDtypeStruct((1, S + 256), jnp.int32),
             ),
             in_specs=[smem] + [hbm] * 7 + [vmem],
-            out_specs=(hbm, hbm, hbm, vmem, vmem),
+            out_specs=(hbm, hbm, hbm, vmem),
             scratch_shapes=[
                 pltpu.VMEM((2, kx_own, ky_own, nz), F32),
                 pltpu.VMEM((2, kx_own, ky_own, nz), F32),
@@ -768,12 +810,14 @@
         )
         energy, density, kelvin, found = pl.pallas_call(
             functools.partial(read_kernel, by),
-            out_shape=(block, block, block, jax.ShapeDtypeStruct((gx * 8, 128), F32)),
-            in_specs=[smem] * 2 + [hbm] * 3,
+            out_shape=(block, block, block, jax.ShapeDtypeStruct((S // 128, 128), F32)),
+            in_specs=[hbm] * 4,
             out_specs=(hbm, hbm, hbm, vmem),
-            scratch_shapes=[pltpu.VMEM((bx, by, bz), F32)] * 3 + [dma((6,))],
-            compiler_params=pltpu.CompilerParams(vmem_limit_bytes=16 * 1024 * 1024),
-        )(code, most, energy, density, kelvin)
+            scratch_shapes=[pltpu.SMEM((1, S + 256), jnp.int32)]
+            + [pltpu.VMEM((bx, by, bz), F32)] * 3
+            + [dma((7,))],
+            compiler_params=pltpu.CompilerParams(vmem_limit_bytes=60 * 1024 * 1024),
+        )(code, energy, density, kelvin)
         model, odds = pl.pallas_call(
             functools.partial(sum_kernel, (gx, gy, gz)),
             out_shape=(
@@ -783,14 +827,15 @@
             in_specs=[smem, vmem, vmem],
             out_specs=(vmem, smem),
             scratch_shapes=[
-                pltpu.VMEM((gx, 8, 128), F32),
-                pltpu.VMEM((gx, 8, 128), F32),
-                pltpu.VMEM((8, 128), F32),
-                pltpu.VMEM((nd, 8, 128), F32),
-                pltpu.VMEM((8, 128), F32),
-                pltpu.VMEM((gx, 8, 128), F32),
-                dma((3,)),
-                dma((3,)),
+                pltpu.VMEM((gz, per, 128), F32),
+                pltpu.VMEM((per, 128), F32),
+                pltpu.VMEM((gx, per, 128), F32),
+                pltpu.VMEM((per, 128), F32),
+                pltpu.VMEM((gy, per, 128), F32),
+                pltpu.VMEM((per, 128), F32),
+                pltpu.VMEM((gz, per, 128), F32),
+                dma((4,)),
+                dma((4,)),
             ],
             compiler_params=pltpu.CompilerParams(collective_id=1, has_side_effects=True),
         )(cost, found, recorded.reshape(S // 128, 128))

time: 129 us -> 119 us (0.922)
  local copies, waits for them, and re-layouts: 6.96 us -> 1.32 us
  Pallas kernels: 118 us -> 114 us
    unnamed x13 -> x1, local copies, waits for them, and re-layouts: 6.96 us -> 1.32 us
    pallas_call x1, Pallas kernels: 9.11 us -> 5.21 us  [body(): pl.pallas_call(functools.partial(read_kernel, by), out_shape=(block, bloc...]
where the time goes in v3:
time: 119 us
  Pallas kernels  114 us (96%)
  between operations  3.69 us (3%)
  local copies, waits for them, and re-layouts  1.32 us (1%)
    pallas_call x1, Pallas kernels, body(): pl.pallas_call(functools.partial(kernel, (gx, gy, gz, nx, ny, nz)), out_s...  86.5 us
    pallas_call x1, Pallas kernels, body(): pl.pallas_call(functools.partial(sum_kernel, (gx, gy, gz)), out_shape=(ja...  22 us
    pallas_call x1, Pallas kernels, body(): pl.pallas_call(functools.partial(read_kernel, by), out_shape=(block, bloc...  5.21 us

profile of v3, /device:TPU:1, one launch (start us, length us, event | category | flops | bytes accessed | tf_op | source)
XLA Modules:
  0.0 118.8 jit_solution(16902706997034543202)
XLA Ops:
  1.3 86.5 %shard_map.146 = (f32[32,64,128]{2,1,0:T(8,128)}, f32[32,64,128]{2,1,0:T(8,128)}, f32[32,64,128]{2,1,0:T(8,128)}, s32[1,4352]{1,0:T(1,128)}) custom-call(f32[1]{0:T(128)S(6)} %copy.18.beta, f32[2,8,64,512]{3,2,1,0:T(8,128)} %inc.1, f32[2,8,64,512]{3,2,1,0:T(8,128)} %ren.1, bf16[8,256,512]{2,1,0:T(8,128)(2,1)} %constant.6.clone.w1_hbm, ...), custom_call_target="tpu_custom_call" | custom-call | flops 7000000000 | bytes 16000000 | tf_op jit(solution)/shard_map/pallas_call | solution.py:748
  87.8 5.2 %shard_map.147 = (f32[32,64,128]{2,1,0:T(8,128)}, f32[32,64,128]{2,1,0:T(8,128)}, f32[32,64,128]{2,1,0:T(8,128)}, f32[32,128]{1,0:T(8,128)}) custom-call(s32[1,4352]{1,0:T(1,128)} %get-tuple-element.15.code_hbm, f32[32,64,128]{2,1,0:T(8,128)} %get-tuple-element.16.thr, f32[32,64,128]{2,1,0:T(8,128)} %get-tuple-element.17.rho, ...), custom_call_target="tpu_custom_call" | custom-call | tf_op jit(solution)/shard_map/pallas_call | solution.py:811
  93.7 22.0 %shard_map.148 = (f32[32,128]{1,0:T(8,128)}, f32[1]{0:T(128)}) custom-call(f32[1]{0:T(128)S(6)} %copy.19.cost, f32[32,128]{1,0:T(8,128)} %get-tuple-element.22.found, f32[32,128]{1,0:T(8,128)} %bitcast.3), custom_call_target="tpu_custom_call" | custom-call | tf_op jit(solution)/shard_map/pallas_call | solution.py:821
  115.7 1.3 %copy.20 = f32[4096]{0:T(1024)} copy(f32[4096]{0:T(1024)} %bitcast.4) | data formatting | bytes 32768

commit v4 on v3

--- a/solution.py
+++ b/solution.py
@@ -19,7 +19,7 @@
 LAG = 3
 GROUPS = 4
 SLOTS = 8
-PIECE = 32
+PIECE = 16
 ABL = set()
 MESH = pl.DeviceIdType.MESH
 F32 = jnp.float32
@@ -154,11 +154,12 @@
     w3_hbm,
     rho0,
     heat0,
-    sensors,
+    sensors_hbm,
     thr_out,
     rho_out,
     heat_out,
     code_out,
+    sensors,
     inc_v,
     ren_v,
     b_high,
@@ -205,6 +206,7 @@
     me = iy * gz + iz
     middle = pl.ds(8, by)
 
+    greet(plane_device, line_device)
     loads = [
         pltpu.make_async_copy(inc, inc_v, load_sem.at[0]),
         pltpu.make_async_copy(ren, ren_v, load_sem.at[1]),
@@ -213,11 +215,10 @@
         pltpu.make_async_copy(rho0, rho_v, load_sem.at[4]),
         pltpu.make_async_copy(w2_hbm, w2, load_sem.at[5]),
         pltpu.make_async_copy(w3_hbm, w3, load_sem.at[6]),
+        pltpu.make_async_copy(sensors_hbm, sensors, load_sem.at[7]),
     ]
     for load in loads:
         load.start()
-    greet(plane_device, line_device)
-
     lane = lax.broadcasted_iota(jnp.int32, (1, 128), 1)
     sign = jnp.where(lane < 64, -1.0, 1.0).astype(F32)
     first_half = lane < 64
@@ -323,7 +324,7 @@
         pltpu.make_async_copy(send3.at[c, iy], target, r3_sem.at[0]).start()
 
     def spot(g, slot):
-        return lax.rem(g * SLOTS + slot + bx - 1, bx)
+        return lax.rem(g * (SLOTS // 2) + slot // 2 + half - 1, half) + slot % 2 * half
 
     near_ones = []
     for number, (place, count) in enumerate([(ix, gx), (iy, gy), (iz, gz)]):
@@ -456,6 +457,11 @@
         return carry
 
     def first_step(g, carry):
+        for slot in range(0, SLOTS, 2):
+            x = spot(g, slot)
+            turned = got3[pl.ds(x, bz, stride=half), :].T
+            thr[x] = turned[:by]
+            thr[half + x] = turned[by:]
         for slot in range(SLOTS):
             x = spot(g, slot)
             rho = rho_v[x]
@@ -464,13 +470,26 @@
             rho = rho + 0.64 * growth
             rho_v[x] = rho
             state[1, 1, x + 1, middle, :] = rho * rho
-        offer(1, g)
 
         @pl.when(g == 0)
         def _():
             offer_ends(1)
 
+        offer(1, g)
         return carry
+
+    def grow(level):
+        def plane(x, carry):
+            rho = rho_v[x]
+            growth = jnp.exp(-thr[x] / state[level, 0, x + 1, middle, :]) * (1.0 - rho)
+            inverse[x] = 0.48 * growth
+            rho = rho + 0.64 * growth
+            rho_v[x] = rho
+            if level + 1 < STEPS:
+                state[level + 1, 1, x + 1, middle, :] = rho * rho
+            return carry
+
+        lax.fori_loop(0, bx, plane, 0, unroll=4)
 
     def later_step(level):
         def group(g, carry):
@@ -482,23 +501,18 @@
             for slot in range(SLOTS):
                 for piece in pieces:
                     x, heat, flux = flux_of(level, g, slot, piece)
-                    rho = rho_v[x - 1, piece, :]
-                    growth = jnp.exp(-thr[x - 1, piece, :] / heat) * (1.0 - rho)
-                    heat = heat + (0.08 * flux + 0.48 * growth)
-                    rho = rho + 0.64 * growth
-                    rho_v[x - 1, piece, :] = rho
+                    heat = heat + (0.08 * flux + inverse[x - 1, piece, :])
                     if level + 1 < STEPS:
-                        rows = pl.ds(8 + piece.start, PIECE)
-                        state[level + 1, 0, x, rows, :] = heat
-                        state[level + 1, 1, x, rows, :] = rho * rho
+                        state[level + 1, 0, x, pl.ds(8 + piece.start, PIECE), :] = heat
                     else:
                         heat_last[x - 1, piece, :] = heat
             if level + 1 < STEPS:
-                offer(level + 1, g)
 
                 @pl.when(g == 0)
                 def _():
                     offer_ends(level + 1)
+
+                offer(level + 1, g)
 
             return carry
 
@@ -514,6 +528,7 @@
         return carry
 
     def locate():
+        loads[7].wait()
         x = sensors[0:1, :] - ix * bx
         y = sensors[1:2, :] - iy * by
         z = sensors[2:3, :] - iz * bz
@@ -570,20 +585,17 @@
     lax.fori_loop(0, CHUNKS + LAG, pipeline, 0)
 
     settle(got3, r3_sem.at[0])
-    for x in range(half):
-        turned = got3[pl.ds(x, bz, stride=half), :].T
-        thr[x] = turned[:by]
-        thr[half + x] = turned[by:]
+    lax.fori_loop(0, GROUPS, first_step, 0)
     thr_copy = pltpu.make_async_copy(thr, thr_out, out_sem.at[0])
     thr_copy.start()
-
-    lax.fori_loop(0, GROUPS, first_step, 0)
+    rho_copy = pltpu.make_async_copy(rho_v, rho_out, out_sem.at[2])
     for level in range(1, STEPS):
+        grow(level)
+        if level + 1 == STEPS:
+            rho_copy.start()
         later_step(level)
     heat_copy = pltpu.make_async_copy(heat_last, heat_out, out_sem.at[1])
-    rho_copy = pltpu.make_async_copy(rho_v, rho_out, out_sem.at[2])
     heat_copy.start()
-    rho_copy.start()
 
     def drain_chunk(c, carry):
         settle(send1.at[c, pl.ds(0, (nd - 1) * part)], s1_sem.at[c])
@@ -627,46 +639,57 @@
         for k, (src, dst) in enumerate(((heat_v, heat_out), (thr_v, thr_out), (rho_v, rho_out)))
     ]
     codes.start()
-    for copy in ins:
+    ins[0].start()
+    lane = lax.broadcasted_iota(jnp.int32, (1, 128), 1)
+    ins[0].wait()
+    outs[0].start()
+    for copy in ins[1:]:
         copy.start()
-    found[...] = jnp.zeros(found.shape, F32)
-    lane = lax.broadcasted_iota(jnp.int32, (1, 128), 1)
-    for copy, after in zip(ins, outs):
+    codes.wait()
+
+    block = heat_v.shape[0] * by * 128
+
+    row_of = lax.broadcasted_iota(jnp.int32, (found.shape[0], 128), 0)
+
+    def fetch(cell, j):
+        place = jnp.right_shift(cell, 7)
+        row = heat_v[jnp.right_shift(place, by.bit_length() - 1), pl.ds(place & (by - 1), 1), :]
+        return pltpu.roll(row, (j - cell) & 127, 1)
+
+    def columns(q, total):
+        for k in range(16):
+            j = 16 * q + k
+            final = code[0, S + j]
+            value = fetch(final & (block - 1), j)
+            number = jnp.right_shift(final, block.bit_length() - 1)
+            total = jnp.where((row_of == number) & (lane == j), value, total)
+        return total
+
+    found[...] = lax.fori_loop(0, 8, columns, jnp.zeros(found.shape, F32))
+
+    for copy, after in zip(ins[1:], outs[1:]):
         copy.wait()
         after.start()
-    codes.wait()
-
-    block = heat_v.shape[0] * by * 128
-
-    def read(t, j):
-        cell = jnp.bitwise_and(code[0, t * 128 + j], block - 1)
-        place = jnp.right_shift(cell, 7)
-        row = heat_v[place // by, pl.ds(lax.rem(place, by), 1), :]
-        turned = pltpu.roll(row, jnp.bitwise_and(j - cell, 127), 1)
-        target = pl.ds(t, 1)
-        found[target, :] = jnp.where(lane == j, turned, found[target, :])
 
     def quad(q, carry):
-        lasts = [code[0, S + 4 * q + t] for t in range(4)]
-
-        @pl.when(functools.reduce(jnp.maximum, lasts) >= 0)
+        counts = [code[0, S + 128 + 4 * q + t] for t in range(4)]
+
+        @pl.when(functools.reduce(jnp.maximum, counts) > 1)
         def _():
             def column(j, carry):
-                final = code[0, S + j]
-
-                @pl.when(final >= 0)
+                @pl.when(code[0, S + 128 + j] > 1)
                 def _():
-                    number = jnp.right_shift(final, block.bit_length() - 1)
-                    alone = code[0, S + 128 + j] == 1
-
                     def one(t, carry):
-                        @pl.when(code[0, t * 128 + j] >= 0)
+                        cell = code[0, t * 128 + j]
+
+                        @pl.when(cell >= 0)
                         def _():
-                            read(t, j)
+                            target = pl.ds(t, 1)
+                            found[target, :] = jnp.where(lane == j, fetch(cell, j), found[target, :])
 
                         return carry
 
-                    lax.fori_loop(jnp.where(alone, number, 0), number + 1, one, 0)
+                    lax.fori_loop(0, jnp.right_shift(code[0, S + j], block.bit_length() - 1), one, 0)
 
                 return carry
 
@@ -680,8 +703,8 @@
 
 
 def sum_kernel(
-    dims, cost, found, recorded, model_out, odds_out, red_a, mid_b, red_b, mid_c, red_c, mid_d,
-    red_d, rs_sem, rr_sem,
+    dims, cost, found_hbm, recorded_hbm, model_out, odds_out, found, recorded, red_a, mid_b, red_b, mid_c, red_c, mid_d,
+    red_d, load_sem, rs_sem, rr_sem,
 ):
     gx, gy, gz = dims
     (ix, iy, iz), _, line_device, row_device = places(gx, gy, gz)
@@ -698,6 +721,13 @@
     def piece(k):
         return pl.ds(pl.multiple_of(k * per, per), per)
 
+    loads = [
+        pltpu.make_async_copy(found_hbm, found, load_sem.at[0]),
+        pltpu.make_async_copy(recorded_hbm, recorded, load_sem.at[1]),
+    ]
+    for load in loads:
+        load.start()
+    loads[0].wait()
     red_a[iz] = found[piece(iz), :]
     pl.semaphore_wait(barrier, len(partners))
     for other, device in quads:
@@ -718,6 +748,7 @@
         remote(mid_d, red_d.at[iz], rs_sem.at[3], rr_sem.at[3], device)
     red_d[iz] = mid_d[...]
     settle(red_d.at[pl.ds(0, gz - 1)], rr_sem.at[3])
+    loads[1].wait()
     values = red_d[...].reshape(S // 128, 128)
     model_out[...] = values
     gap = (values - recorded[...]) / 0.2
@@ -753,9 +784,10 @@
                 block,
                 jax.ShapeDtypeStruct((1, S + 256), jnp.int32),
             ),
-            in_specs=[smem] + [hbm] * 7 + [vmem],
+            in_specs=[smem] + [hbm] * 8,
             out_specs=(hbm, hbm, hbm, vmem),
             scratch_shapes=[
+                pltpu.VMEM((3, S), jnp.int32),
                 pltpu.VMEM((2, kx_own, ky_own, nz), F32),
                 pltpu.VMEM((2, kx_own, ky_own, nz), F32),
                 pltpu.VMEM((kx_own * 2 * ky_own, nz), BF16),
@@ -778,7 +810,7 @@
                 pltpu.VMEM((STEPS, 2, GROUPS, 2, SLOTS, bz), F32),
                 pltpu.VMEM((STEPS, GROUPS, by, bz), F32),
                 pltpu.VMEM((STEPS, 2, GROUPS, by, bz), F32),
-                dma((7,)),
+                dma((8,)),
                 dma((3,)),
                 dma((CHUNKS,)),
                 dma((CHUNKS,)),
@@ -824,9 +856,11 @@
                 jax.ShapeDtypeStruct((S // 128, 128), F32),
                 jax.ShapeDtypeStruct((1,), F32),
             ),
-            in_specs=[smem, vmem, vmem],
+            in_specs=[smem, hbm, hbm],
             out_specs=(vmem, smem),
             scratch_shapes=[
+                pltpu.VMEM((S // 128, 128), F32),
+                pltpu.VMEM((S // 128, 128), F32),
                 pltpu.VMEM((gz, per, 128), F32),
                 pltpu.VMEM((per, 128), F32),
                 pltpu.VMEM((gx, per, 128), F32),
@@ -834,10 +868,13 @@
                 pltpu.VMEM((gy, per, 128), F32),
                 pltpu.VMEM((per, 128), F32),
                 pltpu.VMEM((gz, per, 128), F32),
+                dma((2,)),
                 dma((4,)),
                 dma((4,)),
             ],
-            compiler_params=pltpu.CompilerParams(collective_id=1, has_side_effects=True),
+            compiler_params=pltpu.CompilerParams(
+                collective_id=1, has_side_effects=True, vmem_limit_bytes=60 * 1024 * 1024
+            ),
         )(cost, found, recorded.reshape(S // 128, 128))
         return energy, density, kelvin, model.reshape(S), odds
 

time: 119 us -> 117 us (0.983)
  Pallas kernels: 114 us -> 112 us
    pallas_call x1, Pallas kernels: 86.5 us -> 85.4 us  [body(): pl.pallas_call(functools.partial(kernel, (gx, gy, gz, nx, ny, nz)), out_s...]
where the time goes in v4:
time: 117 us
  Pallas kernels  112 us (96%)
  between operations  3.69 us (3%)
  local copies, waits for them, and re-layouts  1.32 us (1%)
    pallas_call x1, Pallas kernels, body(): pl.pallas_call(functools.partial(kernel, (gx, gy, gz, nx, ny, nz)), out_s...  85.4 us
    pallas_call x1, Pallas kernels, body(): pl.pallas_call(functools.partial(sum_kernel, (gx, gy, gz)), out_shape=(ja...  21.9 us
    pallas_call x1, Pallas kernels, body(): pl.pallas_call(functools.partial(read_kernel, by), out_shape=(block, bloc...  4.81 us

profile of v4, /device:TPU:1, one launch (start us, length us, event | category | flops | bytes accessed | tf_op | source)
XLA Modules:
  0.0 117.1 jit_solution(5781614693301664469)
XLA Ops:
  1.3 85.4 %shard_map.146 = (f32[32,64,128]{2,1,0:T(8,128)}, f32[32,64,128]{2,1,0:T(8,128)}, f32[32,64,128]{2,1,0:T(8,128)}, s32[1,4352]{1,0:T(1,128)}) custom-call(f32[1]{0:T(128)S(6)} %copy.18.beta, f32[2,8,64,512]{3,2,1,0:T(8,128)} %inc.1, f32[2,8,64,512]{3,2,1,0:T(8,128)} %ren.1, bf16[8,256,512]{2,1,0:T(8,128)(2,1)} %constant.6.clone.w1_hbm, ...), custom_call_target="tpu_custom_call" | custom-call | flops 7000000000 | bytes 16000000 | tf_op jit(solution)/shard_map/pallas_call | solution.py:779
  86.6 4.8 %shard_map.147 = (f32[32,64,128]{2,1,0:T(8,128)}, f32[32,64,128]{2,1,0:T(8,128)}, f32[32,64,128]{2,1,0:T(8,128)}, f32[32,128]{1,0:T(8,128)}) custom-call(s32[1,4352]{1,0:T(1,128)} %get-tuple-element.15.code_hbm, f32[32,64,128]{2,1,0:T(8,128)} %get-tuple-element.16.thr, f32[32,64,128]{2,1,0:T(8,128)} %get-tuple-element.17.rho, ...), custom_call_target="tpu_custom_call" | custom-call | tf_op jit(solution)/shard_map/pallas_call | solution.py:843
  92.1 21.9 %shard_map.148 = (f32[32,128]{1,0:T(8,128)}, f32[1]{0:T(128)}) custom-call(f32[1]{0:T(128)S(6)} %copy.19.cost, f32[32,128]{1,0:T(8,128)} %get-tuple-element.22.found_hbm, f32[32,128]{1,0:T(8,128)} %bitcast.3), custom_call_target="tpu_custom_call" | custom-call | tf_op jit(solution)/shard_map/pallas_call | solution.py:853
  114.1 1.3 %copy.20 = f32[4096]{0:T(1024)} copy(f32[4096]{0:T(1024)} %bitcast.4) | data formatting | bytes 32768

commit v5 on v4

--- a/solution.py
+++ b/solution.py
@@ -87,6 +87,7 @@
     if (dx, dy, dc) != (0, 0, 0)
 ]
 LINE_ORDER = [4, 3, -3, 2, -2, 1, -1]
+FAR_FIRST = sorted(PLANE_ORDER, key=lambda o: -min(o[0], 4 - o[0]) - min(o[1], 4 - o[1]))
 ROW_ORDER = [(2, 1), (1, 0), (3, 1), (2, 0), (1, 1), (3, 0), (0, 1)]
 
 
@@ -119,10 +120,11 @@
 
 def greet(plane, line):
     barrier = pltpu.get_barrier_semaphore()
-    for offset in PLANE_ORDER:
-        pl.semaphore_signal(barrier, inc=1, device_id=plane(offset)[1], device_id_type=MESH)
-    for offset in LINE_ORDER:
-        pl.semaphore_signal(barrier, inc=1, device_id=line(offset)[1], device_id_type=MESH)
+    devices = [line(k)[1] for k in LINE_ORDER[:3]]
+    devices += [plane(offset)[1] for offset in FAR_FIRST]
+    devices += [line(k)[1] for k in LINE_ORDER[3:]]
+    for device in devices:
+        pl.semaphore_signal(barrier, inc=1, device_id=device, device_id_type=MESH)
 
 
 def met():
@@ -261,7 +263,7 @@
                 )
 
     def ship1(c):
-        for offset in PLANE_ORDER:
+        for offset in FAR_FIRST:
             other, device = plane_device(offset)
             remote(
                 send1.at[c, pl.ds(other * part, part)],
@@ -703,18 +705,19 @@
 
 
 def sum_kernel(
-    dims, cost, found_hbm, recorded_hbm, model_out, odds_out, found, recorded, red_a, mid_b, red_b, mid_c, red_c, mid_d,
-    red_d, load_sem, rs_sem, rr_sem,
+    dims, cost, found_hbm, recorded_hbm, model_out, odds_out, found, recorded, red_a, mid_b, red_b, mid_c, red_c, load_sem,
+    rs_sem, rr_sem,
 ):
     gx, gy, gz = dims
-    (ix, iy, iz), _, line_device, row_device = places(gx, gy, gz)
+    (ix, iy, iz), plane_device, line_device, _ = places(gx, gy, gz)
+    me = iy * gz + iz
     per = S // 128 // gz
     lines = [line_device(k) for k in LINE_ORDER]
-    rows = [row_device(offset) for offset in ROW_ORDER]
+    planes = [plane_device(offset) for offset in FAR_FIRST]
     quads = [lax.rem(iz + k, gz) for k in (2, 1, 3)]
     quads = [(other, (ix, iy, other)) for other in quads]
     barrier = pltpu.get_barrier_semaphore()
-    partners = lines + rows + quads
+    partners = lines[:3] + planes + lines[3:]
     for _, device in partners:
         pl.semaphore_signal(barrier, inc=1, device_id=device, device_id_type=MESH)
 
@@ -739,24 +742,18 @@
     red_b[ix] = mid_b[...]
     settle(red_b.at[pl.ds(0, gx - 1)], rr_sem.at[1])
     mid_c[...] = jnp.sum(red_b[...], axis=0)
-    for other, device in rows:
-        remote(mid_c, red_c.at[iy], rs_sem.at[2], rr_sem.at[2], device)
-    red_c[iy] = mid_c[...]
-    settle(red_c.at[pl.ds(0, gy - 1)], rr_sem.at[2])
-    mid_d[...] = jnp.sum(red_c[...], axis=0)
-    for other, device in quads:
-        remote(mid_d, red_d.at[iz], rs_sem.at[3], rr_sem.at[3], device)
-    red_d[iz] = mid_d[...]
-    settle(red_d.at[pl.ds(0, gz - 1)], rr_sem.at[3])
+    for _, device in planes:
+        remote(mid_c, red_c.at[me], rs_sem.at[2], rr_sem.at[2], device)
+    red_c[me] = mid_c[...]
+    settle(red_c.at[pl.ds(0, gy * gz - 1)], rr_sem.at[2])
     loads[1].wait()
-    values = red_d[...].reshape(S // 128, 128)
+    values = jnp.sum(red_c[...].reshape(gy, S // 128, 128), axis=0)
     model_out[...] = values
     gap = (values - recorded[...]) / 0.2
     odds_out[0] = cost[0] - 0.5 * (jnp.sum(gap * gap) / S)
     settle(red_a.at[pl.ds(0, gz - 1)], rs_sem.at[0])
     settle(red_b.at[pl.ds(0, gx - 1)], rs_sem.at[1])
-    settle(red_c.at[pl.ds(0, gy - 1)], rs_sem.at[2])
-    settle(red_d.at[pl.ds(0, gz - 1)], rs_sem.at[3])
+    settle(red_c.at[pl.ds(0, gy * gz - 1)], rs_sem.at[2])
 
 
 def solution(mesh):
@@ -865,12 +862,10 @@
                 pltpu.VMEM((per, 128), F32),
                 pltpu.VMEM((gx, per, 128), F32),
                 pltpu.VMEM((per, 128), F32),
-                pltpu.VMEM((gy, per, 128), F32),
-                pltpu.VMEM((per, 128), F32),
-                pltpu.VMEM((gz, per, 128), F32),
+                pltpu.VMEM((nd, per, 128), F32),
                 dma((2,)),
-                dma((4,)),
-                dma((4,)),
+                dma((3,)),
+                dma((3,)),
             ],
             compiler_params=pltpu.CompilerParams(
                 collective_id=1, has_side_effects=True, vmem_limit_bytes=60 * 1024 * 1024

time: 117 us -> 115 us (0.983)
  Pallas kernels: 112 us -> 110 us
    pallas_call x1, Pallas kernels: 21.9 us -> 19.6 us  [body(): pl.pallas_call(functools.partial(sum_kernel, (gx, gy, gz)), out_shape=(ja...]
where the time goes in v5:
time: 115 us
  Pallas kernels  110 us (96%)
  between operations  3.69 us (3%)
  local copies, waits for them, and re-layouts  1.32 us (1%)
    pallas_call x1, Pallas kernels, body(): pl.pallas_call(functools.partial(kernel, (gx, gy, gz, nx, ny, nz)), out_s...  85.3 us
    pallas_call x1, Pallas kernels, body(): pl.pallas_call(functools.partial(sum_kernel, (gx, gy, gz)), out_shape=(ja...  19.6 us
    pallas_call x1, Pallas kernels, body(): pl.pallas_call(functools.partial(read_kernel, by), out_shape=(block, bloc...  4.81 us

profile of v5, /device:TPU:1, one launch (start us, length us, event | category | flops | bytes accessed | tf_op | source)
XLA Modules:
  0.0 114.7 jit_solution(7916685596711179938)
XLA Ops:
  1.3 85.3 %shard_map.146 = (f32[32,64,128]{2,1,0:T(8,128)}, f32[32,64,128]{2,1,0:T(8,128)}, f32[32,64,128]{2,1,0:T(8,128)}, s32[1,4352]{1,0:T(1,128)}) custom-call(f32[1]{0:T(128)S(6)} %copy.18.beta, f32[2,8,64,512]{3,2,1,0:T(8,128)} %inc.1, f32[2,8,64,512]{3,2,1,0:T(8,128)} %ren.1, bf16[8,256,512]{2,1,0:T(8,128)(2,1)} %constant.6.clone.w1_hbm, ...), custom_call_target="tpu_custom_call" | custom-call | flops 7000000000 | bytes 16000000 | tf_op jit(solution)/shard_map/pallas_call | solution.py:776
  86.6 4.8 %shard_map.147 = (f32[32,64,128]{2,1,0:T(8,128)}, f32[32,64,128]{2,1,0:T(8,128)}, f32[32,64,128]{2,1,0:T(8,128)}, f32[32,128]{1,0:T(8,128)}) custom-call(s32[1,4352]{1,0:T(1,128)} %get-tuple-element.15.code_hbm, f32[32,64,128]{2,1,0:T(8,128)} %get-tuple-element.16.thr, f32[32,64,128]{2,1,0:T(8,128)} %get-tuple-element.17.rho, ...), custom_call_target="tpu_custom_call" | custom-call | tf_op jit(solution)/shard_map/pallas_call | solution.py:840
  92.0 19.6 %shard_map.148 = (f32[32,128]{1,0:T(8,128)}, f32[1]{0:T(128)}) custom-call(f32[1]{0:T(128)S(6)} %copy.19.cost, f32[32,128]{1,0:T(8,128)} %get-tuple-element.22.found_hbm, f32[32,128]{1,0:T(8,128)} %bitcast.3), custom_call_target="tpu_custom_call" | custom-call | tf_op jit(solution)/shard_map/pallas_call | solution.py:850
  111.6 1.3 %copy.20 = f32[4096]{0:T(1024)} copy(f32[4096]{0:T(1024)} %bitcast.4) | data formatting | bytes 32768

commit v6 on v5

--- a/solution.py
+++ b/solution.py
@@ -88,7 +88,7 @@
 ]
 LINE_ORDER = [4, 3, -3, 2, -2, 1, -1]
 FAR_FIRST = sorted(PLANE_ORDER, key=lambda o: -min(o[0], 4 - o[0]) - min(o[1], 4 - o[1]))
-ROW_ORDER = [(2, 1), (1, 0), (3, 1), (2, 0), (1, 1), (3, 0), (0, 1)]
+ROW_ORDER = [(2, 1), (1, 1), (3, 1), (2, 0), (0, 1), (1, 0), (3, 0)]
 
 
 def places(gx, gy, gz):

time: 115 us -> 115 us (level)
  no operation moved by 1% of the time
where the time goes in v6:
time: 115 us; the launch traced here: 114 us
  Pallas kernels  109 us (95%)
  between operations  3.69 us (3%)
  local copies, waits for them, and re-layouts  1.32 us (1%)
    pallas_call x1, Pallas kernels, body(): pl.pallas_call(functools.partial(kernel, (gx, gy, gz, nx, ny, nz)), out_s...  85.2 us
    pallas_call x1, Pallas kernels, body(): pl.pallas_call(functools.partial(sum_kernel, (gx, gy, gz)), out_shape=(ja...  19.3 us
    pallas_call x1, Pallas kernels, body(): pl.pallas_call(functools.partial(read_kernel, by), out_shape=(block, bloc...  4.81 us

profile of v6, /device:TPU:1, one launch (start us, length us, event | category | flops | bytes accessed | tf_op | source)
XLA Modules:
  0.0 114.4 jit_solution(15614274345195041243)
XLA Ops:
  1.3 85.2 %shard_map.146 = (f32[32,64,128]{2,1,0:T(8,128)}, f32[32,64,128]{2,1,0:T(8,128)}, f32[32,64,128]{2,1,0:T(8,128)}, s32[1,4352]{1,0:T(1,128)}) custom-call(f32[1]{0:T(128)S(6)} %copy.18.beta, f32[2,8,64,512]{3,2,1,0:T(8,128)} %inc.1, f32[2,8,64,512]{3,2,1,0:T(8,128)} %ren.1, bf16[8,256,512]{2,1,0:T(8,128)(2,1)} %constant.6.clone.w1_hbm, ...), custom_call_target="tpu_custom_call" | custom-call | flops 7000000000 | bytes 16000000 | tf_op jit(solution)/shard_map/pallas_call | solution.py:776
  86.5 4.8 %shard_map.147 = (f32[32,64,128]{2,1,0:T(8,128)}, f32[32,64,128]{2,1,0:T(8,128)}, f32[32,64,128]{2,1,0:T(8,128)}, f32[32,128]{1,0:T(8,128)}) custom-call(s32[1,4352]{1,0:T(1,128)} %get-tuple-element.15.code_hbm, f32[32,64,128]{2,1,0:T(8,128)} %get-tuple-element.16.thr, f32[32,64,128]{2,1,0:T(8,128)} %get-tuple-element.17.rho, ...), custom_call_target="tpu_custom_call" | custom-call | tf_op jit(solution)/shard_map/pallas_call | solution.py:840
  92.0 19.3 %shard_map.148 = (f32[32,128]{1,0:T(8,128)}, f32[1]{0:T(128)}) custom-call(f32[1]{0:T(128)S(6)} %copy.19.cost, f32[32,128]{1,0:T(8,128)} %get-tuple-element.22.found_hbm, f32[32,128]{1,0:T(8,128)} %bitcast.3), custom_call_target="tpu_custom_call" | custom-call | tf_op jit(solution)/shard_map/pallas_call | solution.py:850
  111.3 1.3 %copy.20 = f32[4096]{0:T(1024)} copy(f32[4096]{0:T(1024)} %bitcast.4) | data formatting | bytes 32768
